TPU v7x, 32 devices: a whole 2x2x4 slice. The times are simulated.
32 devices in a mesh: node: 2 (over x), row: 16 (over z, y, core).
Axes of the slice: x: 2, y: 2, z: 4, core: 2. Of those that a mesh axis runs over, the one named last changes fastest.
Arguments:
- hamiltonian: float32 [32, 7, 128, 128], P('row'), may hold values from -0.09375 to 0.09375
- column_blocks: int32 [32, 7], P('row'), may hold values from 0 to 31, as said below
- start_basis: float32 [4096, 256], P('row'), may hold values from -48 to 48
- node_re: float32 [6], P('node'), may hold values from 1.5 to 2.5
- node_im: float32 [6], P('node'), may hold values from 0.5 to 1.5
- weight_re: float32 [6], P('node'), may hold values from 0.5 to 1.5
- weight_im: float32 [6], P('node'), may hold values from -1 to 1
- sweep_count: int32 [6], P('node'), may hold values from 1 to 2, as said below
Outputs:
- basis: float32 [4096, 256], P('row')
Inputs may be any that keep to these rules, and one draw needn't show every extreme that they name: `column_blocks`: tile 0 of row block b lies in column block b, tile 1 in b - 2 and tile 2 in b + 2, taken cyclically modulo 32; every other tile lies within 2 blocks of b, cyclically. `sweep_count`: some node takes 1 sweep and some node takes 2.
All inputs are finite; a program needn't handle non-finite values.
Results may differ from a plain program's by a relative error of at most 0.00022.
Values sent between devices are 32-bit elements; how exact they have to be, the bound alone decides.
No kernel may reach another device: no remote copies, remote signals or barrier semaphores. Data moves between devices by JAX's collectives and lax.ppermute only.
A program may use at most 64 MiB of HBM per device.

v0:
```python
import math

import jax
import jax.numpy as jnp
from jax import lax
from jax.sharding import PartitionSpec as P

REACH = 2
SWEEPS = 2
NS_ITERS = 2


def extended_2(block, sides, width):
    for axis, dim in sides:
        count = lax.axis_size(axis)
        forward = [(i, i + 1) for i in range(count - 1)]
        forward.append((count - 1, 0))
        backward = [(target, source) for source, target in forward]
        low = lax.ppermute(
            lax.slice_in_dim(block, block.shape[dim] - width, None, axis=dim), axis, forward
        )
        high = lax.ppermute(lax.slice_in_dim(block, 0, width, axis=dim), axis, backward)
        block = jnp.concatenate([low, block, high], axis=dim)
    return block


def apply_local(hamiltonian, local_cols, extended):
    breadth = extended.shape[1]
    count_blocks = hamiltonian.shape[0]
    tile_rows = hamiltonian.shape[2]
    blocks = extended.reshape(-1, tile_rows, breadth)
    summed = jnp.zeros((count_blocks, tile_rows, breadth), jnp.float32)
    for column in range(hamiltonian.shape[1]):
        picked = jnp.take(blocks, local_cols[:, column], axis=0)
        summed = summed + jnp.einsum(
            "bij,bjw->biw", hamiltonian[:, column], picked, precision=lax.Precision.HIGHEST
        )
    return summed.reshape(count_blocks * tile_rows, breadth)


def local_gram(vectors):
    return lax.dot_general(
        vectors, vectors, (((0,), (0,)), ((), ())), precision=lax.Precision.HIGHEST
    )


def orthonormal(gram_matrix):
    norm_value = jnp.sqrt(jnp.sum(gram_matrix * gram_matrix) + 1e-06)
    matrix_a = gram_matrix / norm_value
    identity = jnp.eye(gram_matrix.shape[0], dtype=jnp.float32)
    current = identity
    for repeat in range(NS_ITERS):
        middle = 1.5 * identity - 0.5 * jnp.dot(current, matrix_a, precision=lax.Precision.HIGHEST)
        matrix_a = jnp.dot(matrix_a, middle, precision=lax.Precision.HIGHEST)
        current = jnp.dot(middle, current, precision=lax.Precision.HIGHEST)
    return (current, norm_value)


def finish(vectors, gram_matrix, row_scale):
    mixing, norm_value = orthonormal(gram_matrix)
    return (
        row_scale * jnp.dot(vectors, mixing, precision=lax.Precision.HIGHEST) / jnp.sqrt(norm_value)
    )


def on_device(
    hamiltonian, column_blocks, start_basis, node_re, node_im, weight_re, weight_im, sweep_count
):
    count_blocks = hamiltonian.shape[0]
    tile_rows = hamiltonian.shape[2]
    devices_row = lax.axis_size("row")
    first_block = lax.axis_index("row") * count_blocks
    local_cols = (column_blocks - first_block + REACH + count_blocks * devices_row) % (
        count_blocks * devices_row
    )
    rim_rows = REACH * tile_rows
    row_scale = math.sqrt(start_basis.shape[0] * devices_row)
    modulus = node_re * node_re + node_im * node_im
    inverse_re = node_re / modulus
    inverse_im = -node_im / modulus
    power_re, power_im = (inverse_re, inverse_im)
    listed = []
    for degree in range(SWEEPS + 1):
        active = (sweep_count >= degree).astype(jnp.float32)
        listed.append(jnp.sum(active * (weight_re * power_re - weight_im * power_im)))
        power_re, power_im = (
            power_re * inverse_re - power_im * inverse_im,
            power_re * inverse_im + power_im * inverse_re,
        )
    coefficients = lax.psum(jnp.stack(listed), "node")
    krylov = start_basis
    filtered = coefficients[0] * start_basis
    for degree in range(1, SWEEPS + 1):
        extended = extended_2(krylov, (("row", 0),), rim_rows)
        krylov = apply_local(hamiltonian, local_cols, extended)
        filtered = filtered + coefficients[degree] * krylov
    gram_matrix = lax.psum(local_gram(filtered), "row")
    return finish(filtered, gram_matrix, row_scale)


def solution(mesh):
    return jax.shard_map(
        on_device,
        mesh=mesh,
        in_specs=(
            P("row", None, None, None),
            P("row", None),
            P("row", None),
            P("node"),
            P("node"),
            P("node"),
            P("node"),
            P("node"),
        ),
        out_specs=P("row", None),
        check_vma=False,
    )
```

profile of v0, /device:TPU:0, one launch (start us, length us, event | category | flops | bytes accessed | tf_op | source)
XLA Modules:
  0.0 155.2 jit_solution(14468664168108451764)
XLA Ops:
  6.5 0.5 collective-permute-start
  7.0 5.0 %collective-permute-start.1 = (f32[256,256]{1,0:T(8,128)}, f32[256,256]{1,0:T(8,128)S(1)}, u32[]{:S(2)}, u32[]{:S(2)}) collective-permute-start(f32[256,256]{1,0:T(8,128)} %param.12), channel_id=1, source_target_pairs={{1,0},{2,1},{3,2},{4,3},{5,4},{6,5},{7,6},{8,7},{9,8},{10,9},{11,1... | collective-permute-start | bytes 786440 | tf_op jit(solution)/shard_map/ppermute | solution.py:22
  12.0 0.7 copy-done.20
  12.7 0.3 slice_reduce_fusion
  13.0 0.5 compare_and_fusion.6
  13.5 0.6 compare_and_fusion.4
  14.1 0.6 compare_and_fusion.2
  14.7 0.5 compare_and_fusion.1
  15.2 0.6 compare_and_fusion
  15.9 0.6 pad_clamp_fusion.1
  16.5 0.6 pad_clamp_fusion
  17.2 0.5 fusion.82
  17.7 1.0 pad_maximum_fusion
  18.7 0.6 gather_fusion
  19.3 0.6 gather_fusion.1
  19.9 0.6 gather_fusion.2
  20.4 0.6 gather_fusion.3
  21.0 0.6 gather_fusion.4
  21.6 0.7 gather_fusion.5
  22.3 0.7 gather_fusion.6
  23.0 1.1 fusion.18
  24.1 0.6 copy-done.9
  24.7 0.5 convolution_add_fusion.11
  25.2 0.7 copy-done.5
  25.8 0.5 convolution_add_fusion.10
  26.3 0.6 copy-done.11
  27.0 0.5 convolution_add_fusion.9
  27.4 0.7 copy-done.7
  28.1 0.5 convolution_add_fusion.8
  28.7 0.5 convolution_add_fusion.7
  29.4 0.5 convolution_add_fusion.6
  29.9 0.8 collective-permute-start.2
  30.6 3.7 %collective-permute-start.3 = (f32[256,256]{1,0:T(8,128)S(1)}, f32[256,256]{1,0:T(8,128)S(1)}, u32[]{:S(2)}, u32[]{:S(2)}) collective-permute-start(f32[256,256]{1,0:T(8,128)S(1)} %bitcast.90), channel_id=1, source_target_pairs={{1,0},{2,1},{3,2},{4,3},{5,4},{6,5},{7,6},{8,7},{9,8},{10,9},{11,1... | collective-permute-start | bytes 786440 | tf_op jit(solution)/shard_map/ppermute | solution.py:22
  34.4 0.6 copy-done.17
  35.0 0.6 fusion.79
  35.7 1.9 %pad_maximum_fusion.2 = f32[3]{0:T(128)S(1)} fusion(f32[1]{0:T(128)} %bitcast.2, f32[1]{0:T(128)} %bitcast.1, f32[1]{0:T(128)} %bitcast), kind=kLoop, calls=%fused_computation.151 | loop fusion | flops 6 | bytes 24 | tf_op jit(solution)/shard_map/stack | solution.py:90
  37.6 4.9 %psum.14 = f32[3]{0:T(128)S(1)} all-reduce(f32[3]{0:T(128)S(1)} %pad_maximum_fusion.2), channel_id=1, replica_groups=mesh['node'=2,'row'=16] {'node'}, use_global_device_ids=true, to_apply=%region_3.4 | all-reduce | flops 3 | bytes 24 | tf_op jit(solution)/shard_map/psum | solution.py:90
  42.5 0.6 fusion.97
  43.2 0.6 gather_fusion.7
  43.7 0.6 gather_fusion.8
  44.3 0.6 gather_fusion.9
  44.9 0.6 gather_fusion.10
  45.5 0.7 gather_fusion.11
  46.2 0.7 gather_fusion.12
  46.9 1.4 gather_fusion.13
  48.3 0.5 fusion.10
  48.9 0.5 convolution_add_fusion.5
  49.5 0.5 convolution_add_fusion.4
  50.2 0.5 convolution_add_fusion.3
  50.9 0.5 convolution_add_fusion.2
  51.5 0.5 convolution_add_fusion.1
  52.0 0.5 copy-done.2
  52.4 0.2 copy-done.16
  52.6 1.1 fusion.3
  53.7 1.3 bitcast_add_fusion
  55.1 1.3 fusion.98
  56.4 86.6 %all-reduce.2.cloned.1.call-done = f32[256,256]{1,0:T(8,128)} async-done(((f32[256,256]{1,0:T(8,128)}), f32[256,256]{1,0:T(8,128)}) %all-reduce.2.cloned.1.call-update) | async-done | bytes 262160 | tf_op jit(solution)/shard_map/psum | solution.py:97
  143.0 1.7 %multiply_reduce_fusion = f32[]{:T(128)} fusion(f32[256,256]{1,0:T(8,128)} %all-reduce.2.cloned.1.call-done), kind=kLoop, calls=%fused_computation.52 | loop fusion | flops 131071 | bytes 262148 | tf_op jit(solution)/shard_map/reduce_sum | solution.py:48
  145.4 0.3 fusion.2
  145.8 0.3 fusion.20
  146.1 0.4 fusion.77
  146.4 0.4 fusion.1
  146.8 0.4 fusion.99
  147.2 1.1 fusion
  (61 shorter events, 1.5 us)
Async XLA Ops:
  6.5 136.5 %all-reduce.2.cloned.1.call-start = ((), (), s32[]{:S(2)}) async-start(), calls=%async_computation | async-start | bytes 524288 | tf_op jit(solution)/shard_map/psum | solution.py:97
  6.5 11.2 %collective-permute-start = (f32[256,256]{1,0:T(8,128)}, f32[256,256]{1,0:T(8,128)S(1)}, u32[]{:S(2)}, u32[]{:S(2)}) collective-permute-start(f32[256,256]{1,0:T(8,128)} %param.12), channel_id=1, source_target_pairs={{0,1},{1,2},{2,3},{3,4},{4,5},{5,6},{6,7},{7,8},{8,9},{9,10},{10,1... | collective-permute-start | bytes 786440 | tf_op jit(solution)/shard_map/ppermute | solution.py:19
  7.0 10.7 %collective-permute-start.1 = (f32[256,256]{1,0:T(8,128)}, f32[256,256]{1,0:T(8,128)S(1)}, u32[]{:S(2)}, u32[]{:S(2)}) collective-permute-start(f32[256,256]{1,0:T(8,128)} %param.12), channel_id=1, source_target_pairs={{1,0},{2,1},{3,2},{4,3},{5,4},{6,5},{7,6},{8,7},{9,8},{10,9},{11,1... | collective-permute-start | bytes 786440 | tf_op jit(solution)/shard_map/ppermute | solution.py:22
  12.0 0.7 copy-start.20
  15.9 5.1 %copy-start.4 = (s32[1024]{0:T(1024)}, s32[1024]{0:T(1024)S(1)}, u32[]{:S(2)}) copy-start(s32[1024]{0:T(1024)S(1)} %pad_clamp_fusion.2) | copy-start | bytes 12292
  16.5 0.7 copy-start.21
  16.5 0.7 copy-start.22
  21.0 2.0 %copy-start = (f32[2,7,128,128]{3,2,1,0:T(8,128)S(1)}, f32[2,7,128,128]{3,2,1,0:T(8,128)}, u32[]{:S(2)}) copy-start(f32[2,7,128,128]{3,2,1,0:T(8,128)} %param.10) | copy-start | bytes 2752516
  24.1 0.6 copy-start.9
  25.1 0.7 copy-start.5
  26.3 0.7 copy-start.11
  27.4 0.7 copy-start.7
  28.1 0.6 copy-start.13
  28.7 0.7 copy-start.15
  29.4 5.0 %copy-start.24 = (f32[3]{0:T(128)S(1)}, f32[3]{0:T(128)}, u32[]{:S(2)}) copy-start(f32[3]{0:T(128)} %param.16) | copy-start | bytes 40
  29.4 5.0 %copy-start.25 = (f32[3]{0:T(128)S(1)}, f32[3]{0:T(128)}, u32[]{:S(2)}) copy-start(f32[3]{0:T(128)} %param.15) | copy-start | bytes 40
  29.9 13.2 %collective-permute-start.2 = (f32[256,256]{1,0:T(8,128)S(1)}, f32[256,256]{1,0:T(8,128)S(1)}, u32[]{:S(2)}, u32[]{:S(2)}) collective-permute-start(f32[256,256]{1,0:T(8,128)S(1)} %bitcast.89), channel_id=1, source_target_pairs={{0,1},{1,2},{2,3},{3,4},{4,5},{5,6},{6,7},{7,8},{8,9},{9,10},{10,1... | collective-permute-start | bytes 786440 | tf_op jit(solution)/shard_map/ppermute | solution.py:19
  30.6 12.5 %collective-permute-start.3 = (f32[256,256]{1,0:T(8,128)S(1)}, f32[256,256]{1,0:T(8,128)S(1)}, u32[]{:S(2)}, u32[]{:S(2)}) collective-permute-start(f32[256,256]{1,0:T(8,128)S(1)} %bitcast.90), channel_id=1, source_target_pairs={{1,0},{2,1},{3,2},{4,3},{5,4},{6,5},{7,6},{8,7},{9,8},{10,9},{11,1... | collective-permute-start | bytes 786440 | tf_op jit(solution)/shard_map/ppermute | solution.py:22
  34.4 0.6 copy-start.17
  34.4 0.6 copy-start.18
  34.4 0.7 copy-start.23
  46.9 1.4 copy-start.19
  48.3 0.6 copy-start.10
  48.9 0.7 copy-start.6
  49.5 0.7 copy-start.12
  50.2 0.7 copy-start.8
  50.9 0.6 copy-start.14
  51.5 0.9 copy-start.2
  52.0 0.7 copy-start.16
  52.6 1.1 copy-start.1
  143.0 2.4 %copy-start.3 = (f32[256,256]{1,0:T(8,128)S(1)}, f32[256,256]{1,0:T(8,128)}, u32[]{:S(2)}) copy-start(f32[256,256]{1,0:T(8,128)} %all-reduce.2.cloned.1.call-done) | copy-start | bytes 786436
Sparse Core Ops, SparseCore 0:
  56.5 86.4 all-reduce.1
where the time goes:
time: 156 us; the launch traced here: 155 us
  waiting for transfers between devices  86.7 us (56%)
  local copies, waits for them, and re-layouts  16 us (10%)
  between operations  14.6 us (9%)
  matrix products  11.9 us (8%)
  other arithmetic  11.2 us (7%)
  starting transfers between devices  9.94 us (6%)
  blocking collectives  4.92 us (3%)
    psum x1, waiting for transfers between devices, on_device(): gram_matrix = lax.psum(local_gram(filtered), 'row')  86.6 us
    gather x14, local copies, waits for them, and re-layouts, apply_local(): picked = jnp.take(blocks, local_cols[:, column], axis=0)  9.23 us
    ppermute x2, starting transfers between devices, extended_2(): lax.ppermute(lax.slice_in_dim(block, 0, width, axis=dim), axis, backward)  8.71 us
    dot_general x14, matrix products, apply_local(): jnp.einsum('bij,bjw->biw', hamiltonian[:, column], picked, precision=lax....  7.73 us
    unnamed x52, local copies, waits for them, and re-layouts  5.86 us
    psum x1, blocking collectives, on_device(): coefficients = lax.psum(jnp.stack(listed), 'node')  4.92 us
  transfers between devices with their start and end apart: 5, of which 1 were waited for; matrix products, arithmetic and copies ran while one was open for 5% of the time, Pallas kernels for 0%

commit v1 on v0

v1 whole, which is shorter than its diff:
```python
import functools
import math

import jax
import jax.numpy as jnp
from jax import lax
from jax.experimental import pallas as pl
from jax.experimental.pallas import tpu as pltpu
from jax.sharding import PartitionSpec as P

SWEEPS = 2
Z_POLY = (2.25, -2.4375, 1.6875, -0.5625, 0.0625)
SUBLANES = 8

VMEM = pl.BlockSpec(memory_space=pltpu.VMEM)
SMEM = pl.BlockSpec(memory_space=pltpu.SMEM)


def split(x):
    high = x.astype(jnp.bfloat16)
    low = (x - high.astype(jnp.float32)).astype(jnp.bfloat16)
    return high, low


def mm(a, b, dims=((1,), (0,))):
    return lax.dot_general(a, b, (dims, ((), ())), preferred_element_type=jnp.float32)


def mm3(a_high, a_low, b_high, b_low):
    return mm(a_high, b_high) + (mm(a_high, b_low) + mm(a_low, b_high))


def prepare_kernel(total_blocks, cols_ref, ham_ref, high_ref, low_ref, odd_ref, wide):
    count_blocks, stored, tile, _ = ham_ref.shape
    first = cols_ref[0, 0]
    odd = (first // count_blocks) % 2
    odd_ref[...] = jnp.full(odd_ref.shape, odd, jnp.int32)
    wide[...] = jnp.zeros_like(wide)
    for block in range(count_blocks):
        for k in range(stored):
            away = lax.rem(cols_ref[block, k] - first + total_blocks, total_blocks)
            own = away < count_blocks
            right = jnp.logical_and(away >= count_blocks, away < 2 * count_blocks)
            within = jnp.where(
                own, away, jnp.where(right, away - count_blocks, away - total_blocks + count_blocks)
            )
            group = jnp.where(own, 0, jnp.where(right == (odd == 0), 1, 2))
            slot = group * count_blocks + within
            wide[block, slot] += ham_ref[block, k]
    for block in range(count_blocks):
        for slot in range(wide.shape[1]):
            high, low = split(wide[block, slot])
            rows = slice(block * tile, (block + 1) * tile)
            lanes = slice(slot * tile, (slot + 1) * tile)
            high_ref[rows, lanes] = high
            low_ref[rows, lanes] = low


def banded(high_ref, low_ref, parts):
    rows = parts[0].shape[0]
    total = None
    for index, part in enumerate(parts):
        lanes = slice(index * rows, (index + 1) * rows)
        b_high, b_low = split(part[...])
        term = mm3(high_ref[:, lanes], low_ref[:, lanes], b_high, b_low)
        total = term if total is None else total + term
    return total


def sweep_kernel(high_ref, low_ref, own_ref, core_ref, chip_ref, out_ref):
    out_ref[...] = banded(high_ref, low_ref, (own_ref, core_ref, chip_ref))


def gram_kernel(
    high_ref, low_ref, own_ref, core_ref, chip_ref, start_ref, coef_ref, other_ref, odd_ref,
    filtered_ref, mine_ref, theirs_ref,
):
    second = banded(high_ref, low_ref, (own_ref, core_ref, chip_ref))
    coef = coef_ref[...] + other_ref[...]
    filtered = (
        coef[0:1, 0:1] * start_ref[...] + coef[1:2, 0:1] * own_ref[...] + coef[2:3, 0:1] * second
    )
    filtered_ref[...] = filtered
    high, low = split(filtered)
    cross = mm(high, low, ((0,), (0,)))
    gram = mm(high, high, ((0,), (0,))) + (cross + cross.T)
    half = gram.shape[0] // 2
    row = lax.broadcasted_iota(jnp.int32, (half, half), 0)
    col = lax.broadcasted_iota(jnp.int32, (half, half), 1)
    upper, lower, side = gram[:half, :half], gram[half:, half:], gram[:half, half:]
    packed = jnp.where(col >= row, upper, lower)
    diagonal = jnp.sum(jnp.where(col == row, lower, 0.0), axis=0, keepdims=True)
    diagonal = jnp.broadcast_to(diagonal, (SUBLANES, half))
    odd = odd_ref[0:1, 0:1] == 1
    mine_ref[:half] = jnp.where(odd, packed, side)
    theirs_ref[:half] = jnp.where(odd, side, packed)
    mine_ref[half:] = diagonal
    theirs_ref[half:] = diagonal


def finish_kernel(row_scale, filtered_ref, mine_ref, theirs_ref, odd_ref, out_ref):
    half = mine_ref.shape[1]
    odd = odd_ref[0:1, 0:1] == 1
    mine, theirs = mine_ref[...], theirs_ref[...]
    packed = jnp.where(odd, mine, theirs)
    side = jnp.where(odd, theirs, mine)[:half]
    diagonal = packed[half:half + 1]
    packed = packed[:half]
    row = lax.broadcasted_iota(jnp.int32, (half, half), 0)
    col = lax.broadcasted_iota(jnp.int32, (half, half), 1)
    turned = packed.T
    upper = jnp.where(col >= row, packed, turned)
    lower = jnp.where(col < row, packed, jnp.where(col > row, turned, diagonal))
    gram = jnp.concatenate(
        [
            jnp.concatenate([upper, side], axis=1),
            jnp.concatenate([side.T, lower], axis=1),
        ],
        axis=0,
    )
    square = jnp.sum(jnp.sum(gram * gram, axis=0, keepdims=True), axis=1, keepdims=True)
    norm_value = jnp.sqrt(square + 1e-06)
    a = gram / norm_value
    a_high, a_low = split(a)
    a2 = mm3(a_high, a_low, a_high, a_low)
    b_high, b_low = split(a2)
    c_high, c_low = split(Z_POLY[3] * a + Z_POLY[4] * a2)
    rest = Z_POLY[1] * a + Z_POLY[2] * a2 + mm3(b_high, b_low, c_high, c_low)
    z_high, z_low = split(rest)
    filtered = filtered_ref[...]
    f_high, f_low = split(filtered)
    scale = row_scale / jnp.sqrt(norm_value)
    out_ref[...] = scale * (Z_POLY[0] * filtered + mm3(f_high, f_low, z_high, z_low))


def call(kernel, out_shape, n_in, smem=(), scratch=(), flops=0, moved=0, name=None):
    n_out = len(out_shape) if isinstance(out_shape, (tuple, list)) else 1
    return pl.pallas_call(
        kernel,
        out_shape=out_shape,
        in_specs=[SMEM if i in smem else VMEM for i in range(n_in)],
        out_specs=[VMEM] * n_out if isinstance(out_shape, (tuple, list)) else VMEM,
        scratch_shapes=scratch,
        cost_estimate=pl.CostEstimate(flops=flops, bytes_accessed=moved, transcendentals=0),
        compiler_params=pltpu.CompilerParams(vmem_limit_bytes=24 * 2**20),
        name=name,
    )


def on_device(
    hamiltonian, column_blocks, start_basis, node_re, node_im, weight_re, weight_im, sweep_count
):
    f32 = jnp.float32
    count_blocks, stored, tile, _ = hamiltonian.shape
    rows, vecs = start_basis.shape
    devices = lax.axis_size("row")
    nodes = lax.axis_size("node")
    row_scale = math.sqrt(rows * devices)

    core_pairs = [(i, i ^ 1) for i in range(devices)]
    chip_pairs = [(i, (i + (1 if i % 2 else -1)) % devices) for i in range(devices)]

    def halo(block):
        chip = lax.ppermute(block, "row", chip_pairs)
        core = lax.ppermute(block, "row", core_pairs)
        return core, chip

    modulus = node_re * node_re + node_im * node_im
    inverse_re = node_re / modulus
    inverse_im = -node_im / modulus
    power_re, power_im = inverse_re, inverse_im
    listed = []
    for degree in range(SWEEPS + 1):
        active = (sweep_count >= degree).astype(f32)
        listed.append(jnp.sum(active * (weight_re * power_re - weight_im * power_im)))
        power_re, power_im = (
            power_re * inverse_re - power_im * inverse_im,
            power_re * inverse_im + power_im * inverse_re,
        )
    listed += [jnp.zeros((), f32)] * (SUBLANES - len(listed))
    coef = jnp.broadcast_to(jnp.stack(listed)[:, None], (SUBLANES, 128))

    start_core, start_chip = halo(start_basis)
    wide = rows * 3
    high, low, odd = call(
        functools.partial(prepare_kernel, count_blocks * devices),
        (
            jax.ShapeDtypeStruct((rows, wide), jnp.bfloat16),
            jax.ShapeDtypeStruct((rows, wide), jnp.bfloat16),
            jax.ShapeDtypeStruct((SUBLANES, 128), jnp.int32),
        ),
        2,
        smem=(0,),
        scratch=[pltpu.VMEM((count_blocks, 3 * count_blocks, tile, tile), f32)],
        flops=hamiltonian.size * 4,
        moved=hamiltonian.size * 4 + rows * wide * 8,
        name="prepare",
    )(column_blocks, hamiltonian)

    other = coef
    for shift in range(1, nodes):
        moved = lax.ppermute(coef, "node", [(i, i ^ shift) for i in range(nodes)])
        other = moved if shift == 1 else other + moved

    first = call(
        sweep_kernel,
        jax.ShapeDtypeStruct((rows, vecs), f32),
        5,
        flops=6 * rows * wide * vecs,
        moved=rows * wide * 4 + 16 * rows * vecs,
        name="sweep",
    )(high, low, start_basis, start_core, start_chip)
    first_core, first_chip = halo(first)

    half = vecs // 2
    part = jax.ShapeDtypeStruct((half + SUBLANES, half), f32)
    filtered, mine, theirs = call(
        gram_kernel,
        (jax.ShapeDtypeStruct((rows, vecs), f32), part, part),
        9,
        flops=6 * rows * wide * vecs + 4 * rows * vecs * vecs,
        moved=rows * wide * 4 + 20 * rows * vecs,
        name="gram",
    )(high, low, first, first_core, first_chip, start_basis, coef, other, odd)

    total = mine + lax.ppermute(theirs, "row", core_pairs)
    step = 2
    while step < devices:
        total = total + lax.ppermute(total, "row", [(i, i ^ step) for i in range(devices)])
        step *= 2
    theirs = lax.ppermute(total, "row", core_pairs)

    return call(
        functools.partial(finish_kernel, row_scale),
        jax.ShapeDtypeStruct((rows, vecs), f32),
        4,
        flops=18 * vecs**3,
        moved=8 * rows * vecs + 4 * vecs * vecs,
        name="finish",
    )(filtered, total, theirs, odd)


def solution(mesh):
    return jax.shard_map(
        on_device,
        mesh=mesh,
        in_specs=(
            P("row", None, None, None),
            P("row", None),
            P("row", None),
            P("node"),
            P("node"),
            P("node"),
            P("node"),
            P("node"),
        ),
        out_specs=P("row", None),
        check_vma=False,
    )
```

time: 156 us -> 41.7 us (0.27)
  waiting for transfers between devices: 86.7 us -> 20.1 us
  between operations: 14.6 us -> 0.13 us
  matrix products: 11.9 us -> 0 us
  local copies, waits for them, and re-layouts: 16 us -> 4.53 us
  other arithmetic: 11.2 us -> 0.69 us
  blocking collectives: 4.92 us -> 0 us
  Pallas kernels: 0 us -> 4.09 us
  starting transfers between devices: 9.94 us -> 11.9 us
    psum x1 -> x0, waiting for transfers between devices: 86.6 us -> none  [on_device(): gram_matrix = lax.psum(local_gram(filtered), 'row')]
    ppermute x4 -> x10, waiting for transfers between devices: 0.01 us -> 20.1 us  [the longest x3 13.8 us: on_device(): lax.ppermute(total, 'row', [(i, i ^ step) for i in range(devices)])]
    dot_general x21 -> x0, matrix products: 11.9 us -> none  [the longest x14 7.73 us: apply_local(): jnp.einsum('bij,bjw->biw', hamiltonian[:, column], picked, precision=lax....]
    gather x14 -> x0, local copies, waits for them, and re-layouts: 9.23 us -> none  [apply_local(): picked = jnp.take(blocks, local_cols[:, column], axis=0)]
    psum x1 -> x0, blocking collectives: 4.92 us -> none  [on_device(): coefficients = lax.psum(jnp.stack(listed), 'node')]
    pallas_call x0 -> x4, Pallas kernels: none -> 4.09 us  [the longest x1 1.88 us: on_device(): call(functools.partial(finish_kernel, row_scale), jax.ShapeDtypeStruct((r...]
    unnamed x52 -> x16, local copies, waits for them, and re-layouts: 5.86 us -> 2.54 us
    and x5 -> x0, other arithmetic: 2.82 us -> none  [apply_local(): picked = jnp.take(blocks, local_cols[:, column], axis=0)]
  transfers between devices with their start and end apart: 5 -> 10, of which waited for: 1 -> 7; matrix products, arithmetic and copies ran while one was open for 5% -> 6% of each run, Pallas kernels for 0% -> 2%
where the time goes in v1:
time: 41.7 us; the launch traced here: 41.5 us
  waiting for transfers between devices  20.1 us (48%)
  starting transfers between devices  11.9 us (29%)
  local copies, waits for them, and re-layouts  4.53 us (11%)
  Pallas kernels  4.09 us (10%)
  other arithmetic  0.69 us (2%)
    ppermute x3, waiting for transfers between devices, on_device(): lax.ppermute(total, 'row', [(i, i ^ step) for i in range(devices)])  13.8 us
    ppermute x2, starting transfers between devices, halo(): chip = lax.ppermute(block, 'row', chip_pairs)  9.87 us
    unnamed x16, local copies, waits for them, and re-layouts  2.54 us
    ppermute x1, waiting for transfers between devices, on_device(): moved = lax.ppermute(coef, 'node', [(i, i ^ shift) for i in range(nodes)])  2.11 us
    another operation x1, local copies, waits for them, and re-layouts, on_device(): coef = jnp.broadcast_to(jnp.stack(listed)[:, None], (SUBLANES, 128))  1.92 us
    pallas_call x1, Pallas kernels, on_device(): call(functools.partial(finish_kernel, row_scale), jax.ShapeDtypeStruct((r...  1.88 us
    ppermute x2, waiting for transfers between devices, halo(): chip = lax.ppermute(block, 'row', chip_pairs)  1.72 us
    ppermute x1, starting transfers between devices, on_device(): moved = lax.ppermute(coef, 'node', [(i, i ^ shift) for i in range(nodes)])  1.5 us
  transfers between devices with their start and end apart: 10, of which 7 were waited for; matrix products, arithmetic and copies ran while one was open for 6% of the time, Pallas kernels for 2%

profile of v1, /device:TPU:0, one launch (start us, length us, event | category | flops | bytes accessed | tf_op | source)
XLA Modules:
  0.0 41.5 jit_solution(2388825054620770725)
XLA Ops:
  0.0 0.0 copy-start
  0.0 5.4 %collective-permute-start.1 = (f32[256,256]{1,0:T(8,128)}, f32[256,256]{1,0:T(8,128)S(1)}, u32[]{:S(2)}, u32[]{:S(2)}) collective-permute-start(f32[256,256]{1,0:T(8,128)} %start_ref.1), channel_id=1, source_target_pairs={{0,15},{1,2},{2,1},{3,4},{4,3},{5,6},{6,5},{7,8},{8,7},{9,10},{10,... | collective-permute-start | bytes 786440 | tf_op jit(solution)/shard_map/ppermute | solution.py:164
  5.4 0.0 collective-permute-start
  5.5 0.0 copy-start.1
  5.5 1.2 %copy-done.1 = f32[2,7,128,128]{3,2,1,0:T(8,128)S(1)} copy-done((f32[2,7,128,128]{3,2,1,0:T(8,128)S(1)}, f32[2,7,128,128]{3,2,1,0:T(8,128)}, u32[]{:S(2)}) %copy-start.1) | copy-done | bytes 917528
  6.6 0.0 copy-start.2
  6.6 0.7 %copy-done.2 = s32[2,7]{1,0:T(2,128)S(1)} copy-done((s32[2,7]{1,0:T(2,128)S(1)}, s32[2,7]{1,0:T(2,128)}, u32[]{:S(2)}) %copy-start.2) | copy-done | bytes 80
  7.3 0.9 %prepare.1 = (bf16[256,768]{1,0:T(8,128)(2,1)S(1)}, bf16[256,768]{1,0:T(8,128)(2,1)S(1)}, s32[8,128]{1,0:T(8,128)S(1)}) custom-call(s32[2,7]{1,0:T(2,128)S(1)} %copy-done.2, f32[2,7,128,128]{3,2,1,0:T(8,128)S(1)} %copy-done.1), custom_call_target="tpu_custom_call" | custom-call | flops 917504 | bytes 2490368 | tf_op jit(solution)/shard_map/prepare/pallas_call | solution.py:185
  8.2 1.7 %collective-permute-done.1.chip_ref = f32[256,256]{1,0:T(8,128)S(1)} collective-permute-done((f32[256,256]{1,0:T(8,128)}, f32[256,256]{1,0:T(8,128)S(1)}, u32[]{:S(2)}, u32[]{:S(2)}) %collective-permute-start.1) | collective-permute-done | bytes 262176 | tf_op jit(solution)/shard_map/ppermute | solution.py:164
  9.9 0.0 collective-permute-done.core_ref
  9.9 0.0 copy-done
  9.9 0.0 copy-start.3
  9.9 0.0 copy-start.4
  9.9 0.5 %sweep.1.own_ref = f32[256,256]{1,0:T(8,128)S(1)} custom-call(bf16[256,768]{1,0:T(8,128)(2,1)S(1)} %get-tuple-element.11.high_ref, bf16[256,768]{1,0:T(8,128)(2,1)S(1)} %get-tuple-element.12.low_ref, f32[256,256]{1,0:T(8,128)S(1)} %copy-done, f32[256,256]{1,0:T(8,128)S(1)} %collective-permute-done.core_ref, f32[256,256]{1,0:T(8,128)S(1)} %collective-permute-done.1.chip_ref), custom_call_target="tpu_custom_call" | custom-call | flops 301989888 | bytes 1835008 | tf_op jit(solution)/shard_map/sweep/pallas_call | solution.py:205
  10.4 4.4 %collective-permute-start.3 = (f32[256,256]{1,0:T(8,128)S(1)}, f32[256,256]{1,0:T(8,128)S(1)}, u32[]{:S(2)}, u32[]{:S(2)}) collective-permute-start(f32[256,256]{1,0:T(8,128)S(1)} %sweep.1.own_ref), channel_id=1, source_target_pairs={{0,15},{1,2},{2,1},{3,4},{4,3},{5,6},{6,5},{7,8},{8,7},{9,10},{10,... | collective-permute-start | bytes 786440 | tf_op jit(solution)/shard_map/ppermute | solution.py:164
  14.8 0.0 collective-permute-start.2
  14.8 0.0 copy-done.3
  14.8 0.0 copy-done.4
  14.9 0.0 copy-start.5
  14.9 0.0 copy-start.6
  14.9 0.0 copy-start.7
  14.9 0.6 %copy-done.5 = s32[3]{0:T(128)S(1)} copy-done((s32[3]{0:T(128)S(1)}, s32[3]{0:T(128)}, u32[]{:S(2)}) %copy-start.5) | copy-done | bytes 36
  15.5 0.0 copy-done.6
  15.5 0.0 copy-done.7
  15.6 0.6 %fusion.2 = (f32[]{:T(128)}, f32[]{:T(128)}, f32[]{:T(128)}) fusion(s32[3]{0:T(128)S(1)} %copy-done.5, f32[3]{0:T(128)S(1)} %copy-done.6, f32[3]{0:T(128)S(1)} %get-tuple-element.21, f32[3]{0:T(128)S(1)} %get-tuple-element.20, f32[3]{0:T(128)S(1)} %copy-done.7), kind=kLoop, calls=%fused_computation.5 | loop fusion | flops 84 | bytes 72 | tf_op jit(solution)/shard_map/reduce_sum | solution.py:175
  16.2 1.9 %stack.15 = f32[8]{0:T(128)S(1)} concatenate(f32[1]{0:T(128)} %bitcast, f32[1]{0:T(128)} %bitcast.1, f32[1]{0:T(128)} %bitcast.2, f32[1]{0:T(128)} %constant.13.clone.1, f32[4]{0:T(128)S(1)} %broadcast.22), dimensions={0} | concatenate | bytes 64 | tf_op jit(solution)/shard_map/stack | solution.py:181
  18.1 0.1 broadcast_in_dim.2.coef_ref
  18.2 1.5 %collective-permute-start.4 = (f32[8,128]{1,0:T(8,128)S(1)}, f32[8,128]{1,0:T(8,128)S(1)}, u32[]{:S(2)}, u32[]{:S(2)}) collective-permute-start(f32[8,128]{1,0:T(8,128)S(1)} %broadcast_in_dim.2.coef_ref), channel_id=1, source_target_pairs={{0,16},{16,0},{1,17},{17,1},{2,18},{18,2},{3,19},{19,3},{4,20},{20... | collective-permute-start | bytes 12296 | tf_op jit(solution)/shard_map/ppermute | solution.py:202
  19.7 2.1 %collective-permute-done.4.other_ref = f32[8,128]{1,0:T(8,128)S(1)} collective-permute-done((f32[8,128]{1,0:T(8,128)S(1)}, f32[8,128]{1,0:T(8,128)S(1)}, u32[]{:S(2)}, u32[]{:S(2)}) %collective-permute-start.4) | collective-permute-done | bytes 4128 | tf_op jit(solution)/shard_map/ppermute | solution.py:202
  21.8 0.0 collective-permute-done.3.chip_ref
  21.8 0.0 collective-permute-done.2.core_ref
  21.8 0.9 %gram.1 = (f32[256,256]{1,0:T(8,128)S(1)}, f32[136,128]{1,0:T(8,128)S(1)}, f32[136,128]{1,0:T(8,128)S(1)}) custom-call(bf16[256,768]{1,0:T(8,128)(2,1)S(1)} %get-tuple-element.11.high_ref, bf16[256,768]{1,0:T(8,128)(2,1)S(1)} %get-tuple-element.12.low_ref, f32[256,256]{1,0:T(8,128)S(1)} %sweep.1.own_ref, f32[256,256]{1,0:T(8,128)S(1)} %collective-permute-done.2.core_ref, ...), custom_call_target="tpu_custom_call" | custom-call | flops 369098752 | bytes 2097152 | tf_op jit(solution)/shard_map/gram/pallas_call | solution.py:217
  22.7 0.1 collective-permute-start.5
  22.8 1.2 %collective-permute-done.5 = f32[136,128]{1,0:T(8,128)S(1)} collective-permute-done((f32[136,128]{1,0:T(8,128)S(1)}, f32[136,128]{1,0:T(8,128)S(1)}, u32[]{:S(2)}, u32[]{:S(2)}) %collective-permute-start.5) | collective-permute-done | bytes 69664 | tf_op jit(solution)/shard_map/ppermute | solution.py:226
  24.0 0.1 collective-permute-start.6
  24.1 4.3 %collective-permute-done.6 = f32[136,128]{1,0:T(8,128)S(1)} collective-permute-done((f32[136,128]{1,0:T(8,128)S(1)}, f32[136,128]{1,0:T(8,128)S(1)}, u32[]{:S(2)}, u32[]{:S(2)}) %collective-permute-start.6) | collective-permute-done | bytes 69664 | tf_op jit(solution)/shard_map/ppermute | solution.py:229
  28.4 0.1 collective-permute-start.7
  28.5 4.3 %collective-permute-done.7 = f32[136,128]{1,0:T(8,128)S(1)} collective-permute-done((f32[136,128]{1,0:T(8,128)S(1)}, f32[136,128]{1,0:T(8,128)S(1)}, u32[]{:S(2)}, u32[]{:S(2)}) %collective-permute-start.7) | collective-permute-done | bytes 69664 | tf_op jit(solution)/shard_map/ppermute | solution.py:229
  32.8 0.3 collective-permute-start.8
  33.1 5.2 %collective-permute-done.8 = f32[136,128]{1,0:T(8,128)S(1)} collective-permute-done((f32[136,128]{1,0:T(8,128)S(1)}, f32[136,128]{1,0:T(8,128)S(1)}, u32[]{:S(2)}, u32[]{:S(2)}) %collective-permute-start.8) | collective-permute-done | bytes 69664 | tf_op jit(solution)/shard_map/ppermute | solution.py:229
  38.3 0.1 collective-permute-start.9
  38.3 1.2 %collective-permute-done.9.theirs_ref = f32[136,128]{1,0:T(8,128)S(1)} collective-permute-done((f32[136,128]{1,0:T(8,128)S(1)}, f32[136,128]{1,0:T(8,128)S(1)}, u32[]{:S(2)}, u32[]{:S(2)}) %collective-permute-start.9) | collective-permute-done | bytes 69664 | tf_op jit(solution)/shard_map/ppermute | solution.py:231
  39.6 1.9 %finish.1 = f32[256,256]{1,0:T(8,128)} custom-call(f32[256,256]{1,0:T(8,128)S(1)} %get-tuple-element.14.filtered_ref, f32[136,128]{1,0:T(8,128)S(1)} %add.27.mine_ref, f32[136,128]{1,0:T(8,128)S(1)} %collective-permute-done.9.theirs_ref, s32[8,128]{1,0:T(8,128)S(1)} %get-tuple-element.13.odd_ref), custom_call_target="tpu_custom_call" | custom-call | flops 301989888 | bytes 786432 | tf_op jit(solution)/shard_map/finish/pallas_call | solution.py:233
  (6 shorter events, 0.0 us)
Async XLA Ops:
  0.0 9.9 %copy-start = (f32[256,256]{1,0:T(8,128)S(1)}, f32[256,256]{1,0:T(8,128)}, u32[]{:S(2)}) copy-start(f32[256,256]{1,0:T(8,128)} %start_ref.1) | copy-start | bytes 786436
  0.0 9.9 %collective-permute-start.1 = (f32[256,256]{1,0:T(8,128)}, f32[256,256]{1,0:T(8,128)S(1)}, u32[]{:S(2)}, u32[]{:S(2)}) collective-permute-start(f32[256,256]{1,0:T(8,128)} %start_ref.1), channel_id=1, source_target_pairs={{0,15},{1,2},{2,1},{3,4},{4,3},{5,6},{6,5},{7,8},{8,7},{9,10},{10,... | collective-permute-start | bytes 786440 | tf_op jit(solution)/shard_map/ppermute | solution.py:164
  5.4 4.4 %collective-permute-start = (f32[256,256]{1,0:T(8,128)}, f32[256,256]{1,0:T(8,128)S(1)}, u32[]{:S(2)}, u32[]{:S(2)}) collective-permute-start(f32[256,256]{1,0:T(8,128)} %start_ref.1), channel_id=1, source_target_pairs={{0,1},{1,0},{2,3},{3,2},{4,5},{5,4},{6,7},{7,6},{8,9},{9,8},{10,11... | collective-permute-start | bytes 786440 | tf_op jit(solution)/shard_map/ppermute | solution.py:165
  5.5 1.2 %copy-start.1 = (f32[2,7,128,128]{3,2,1,0:T(8,128)S(1)}, f32[2,7,128,128]{3,2,1,0:T(8,128)}, u32[]{:S(2)}) copy-start(f32[2,7,128,128]{3,2,1,0:T(8,128)} %ham_ref.1) | copy-start | bytes 2752516
  6.6 0.7 %copy-start.2 = (s32[2,7]{1,0:T(2,128)S(1)}, s32[2,7]{1,0:T(2,128)}, u32[]{:S(2)}) copy-start(s32[2,7]{1,0:T(2,128)} %cols_ref.1) | copy-start | bytes 172
  9.9 4.9 %copy-start.3 = (f32[3]{0:T(128)S(1)}, f32[3]{0:T(128)}, u32[]{:S(2)}) copy-start(f32[3]{0:T(128)} %param.12) | copy-start | bytes 40
  9.9 4.9 %copy-start.4 = (f32[3]{0:T(128)S(1)}, f32[3]{0:T(128)}, u32[]{:S(2)}) copy-start(f32[3]{0:T(128)} %param.11) | copy-start | bytes 40
  10.4 11.4 %collective-permute-start.3 = (f32[256,256]{1,0:T(8,128)S(1)}, f32[256,256]{1,0:T(8,128)S(1)}, u32[]{:S(2)}, u32[]{:S(2)}) collective-permute-start(f32[256,256]{1,0:T(8,128)S(1)} %sweep.1.own_ref), channel_id=1, source_target_pairs={{0,15},{1,2},{2,1},{3,4},{4,3},{5,6},{6,5},{7,8},{8,7},{9,10},{10,... | collective-permute-start | bytes 786440 | tf_op jit(solution)/shard_map/ppermute | solution.py:164
  14.8 7.0 %collective-permute-start.2 = (f32[256,256]{1,0:T(8,128)S(1)}, f32[256,256]{1,0:T(8,128)S(1)}, u32[]{:S(2)}, u32[]{:S(2)}) collective-permute-start(f32[256,256]{1,0:T(8,128)S(1)} %sweep.1.own_ref), channel_id=1, source_target_pairs={{0,1},{1,0},{2,3},{3,2},{4,5},{5,4},{6,7},{7,6},{8,9},{9,8},{10,11... | collective-permute-start | bytes 786440 | tf_op jit(solution)/shard_map/ppermute | solution.py:165
  14.9 0.7 %copy-start.5 = (s32[3]{0:T(128)S(1)}, s32[3]{0:T(128)}, u32[]{:S(2)}) copy-start(s32[3]{0:T(128)} %param.15) | copy-start | bytes 40
  14.9 0.7 %copy-start.6 = (f32[3]{0:T(128)S(1)}, f32[3]{0:T(128)}, u32[]{:S(2)}) copy-start(f32[3]{0:T(128)} %param.14) | copy-start | bytes 40
  14.9 0.7 %copy-start.7 = (f32[3]{0:T(128)S(1)}, f32[3]{0:T(128)}, u32[]{:S(2)}) copy-start(f32[3]{0:T(128)} %param.13) | copy-start | bytes 40
  18.2 3.6 %collective-permute-start.4 = (f32[8,128]{1,0:T(8,128)S(1)}, f32[8,128]{1,0:T(8,128)S(1)}, u32[]{:S(2)}, u32[]{:S(2)}) collective-permute-start(f32[8,128]{1,0:T(8,128)S(1)} %broadcast_in_dim.2.coef_ref), channel_id=1, source_target_pairs={{0,16},{16,0},{1,17},{17,1},{2,18},{18,2},{3,19},{19,3},{4,20},{20... | collective-permute-start | bytes 12296 | tf_op jit(solution)/shard_map/ppermute | solution.py:202
  22.7 1.3 %collective-permute-start.5 = (f32[136,128]{1,0:T(8,128)S(1)}, f32[136,128]{1,0:T(8,128)S(1)}, u32[]{:S(2)}, u32[]{:S(2)}) collective-permute-start(f32[136,128]{1,0:T(8,128)S(1)} %get-tuple-element.16), channel_id=1, source_target_pairs={{0,1},{1,0},{2,3},{3,2},{4,5},{5,4},{6,7},{7,6},{8,9},{9,8},{10,11... | collective-permute-start | bytes 208904 | tf_op jit(solution)/shard_map/ppermute | solution.py:226
  24.0 4.4 %collective-permute-start.6 = (f32[136,128]{1,0:T(8,128)S(1)}, f32[136,128]{1,0:T(8,128)S(1)}, u32[]{:S(2)}, u32[]{:S(2)}) collective-permute-start(f32[136,128]{1,0:T(8,128)S(1)} %add.24), channel_id=1, source_target_pairs={{0,2},{1,3},{2,0},{3,1},{4,6},{5,7},{6,4},{7,5},{8,10},{9,11},{10,... | collective-permute-start | bytes 208904 | tf_op jit(solution)/shard_map/ppermute | solution.py:229
  28.4 4.4 %collective-permute-start.7 = (f32[136,128]{1,0:T(8,128)S(1)}, f32[136,128]{1,0:T(8,128)S(1)}, u32[]{:S(2)}, u32[]{:S(2)}) collective-permute-start(f32[136,128]{1,0:T(8,128)S(1)} %add.25), channel_id=1, source_target_pairs={{0,4},{1,5},{2,6},{3,7},{4,0},{5,1},{6,2},{7,3},{8,12},{9,13},{10,... | collective-permute-start | bytes 208904 | tf_op jit(solution)/shard_map/ppermute | solution.py:229
  32.8 5.5 %collective-permute-start.8 = (f32[136,128]{1,0:T(8,128)S(1)}, f32[136,128]{1,0:T(8,128)S(1)}, u32[]{:S(2)}, u32[]{:S(2)}) collective-permute-start(f32[136,128]{1,0:T(8,128)S(1)} %add.26), channel_id=1, source_target_pairs={{0,8},{1,9},{2,10},{3,11},{4,12},{5,13},{6,14},{7,15},{8,0},{9,1},... | collective-permute-start | bytes 208904 | tf_op jit(solution)/shard_map/ppermute | solution.py:229
  38.3 1.3 %collective-permute-start.9 = (f32[136,128]{1,0:T(8,128)S(1)}, f32[136,128]{1,0:T(8,128)S(1)}, u32[]{:S(2)}, u32[]{:S(2)}) collective-permute-start(f32[136,128]{1,0:T(8,128)S(1)} %add.27.mine_ref), channel_id=1, source_target_pairs={{0,1},{1,0},{2,3},{3,2},{4,5},{5,4},{6,7},{7,6},{8,9},{9,8},{10,11... | collective-permute-start | bytes 208904 | tf_op jit(solution)/shard_map/ppermute | solution.py:231

commit v2 on v1

--- a/solution.py
+++ b/solution.py
@@ -30,7 +30,13 @@
     return mm(a_high, b_high) + (mm(a_high, b_low) + mm(a_low, b_high))
 
 
-def prepare_kernel(total_blocks, cols_ref, ham_ref, high_ref, low_ref, odd_ref, wide):
+def prepare_kernel(total_blocks, cols_ref, *refs):
+    shares, (ham_ref, high_ref, low_ref, odd_ref, coef_ref, wide) = refs[:-6], refs[-6:]
+    row = lax.broadcasted_iota(jnp.int32, coef_ref.shape, 0)
+    coef = jnp.zeros(coef_ref.shape, jnp.float32)
+    for degree, share in enumerate(shares):
+        coef = jnp.where(row == degree, jnp.sum(share[...], axis=1, keepdims=True), coef)
+    coef_ref[...] = coef
     count_blocks, stored, tile, _ = ham_ref.shape
     first = cols_ref[0, 0]
     odd = (first // count_blocks) % 2
@@ -172,35 +178,28 @@
     listed = []
     for degree in range(SWEEPS + 1):
         active = (sweep_count >= degree).astype(f32)
-        listed.append(jnp.sum(active * (weight_re * power_re - weight_im * power_im)))
+        listed.append((active * (weight_re * power_re - weight_im * power_im))[None, :])
         power_re, power_im = (
             power_re * inverse_re - power_im * inverse_im,
             power_re * inverse_im + power_im * inverse_re,
         )
-    listed += [jnp.zeros((), f32)] * (SUBLANES - len(listed))
-    coef = jnp.broadcast_to(jnp.stack(listed)[:, None], (SUBLANES, 128))
-
     start_core, start_chip = halo(start_basis)
     wide = rows * 3
-    high, low, odd = call(
+    high, low, odd, coef = call(
         functools.partial(prepare_kernel, count_blocks * devices),
         (
             jax.ShapeDtypeStruct((rows, wide), jnp.bfloat16),
             jax.ShapeDtypeStruct((rows, wide), jnp.bfloat16),
             jax.ShapeDtypeStruct((SUBLANES, 128), jnp.int32),
+            jax.ShapeDtypeStruct((SUBLANES, 128), f32),
         ),
-        2,
+        2 + len(listed),
         smem=(0,),
         scratch=[pltpu.VMEM((count_blocks, 3 * count_blocks, tile, tile), f32)],
         flops=hamiltonian.size * 4,
         moved=hamiltonian.size * 4 + rows * wide * 8,
         name="prepare",
-    )(column_blocks, hamiltonian)
-
-    other = coef
-    for shift in range(1, nodes):
-        moved = lax.ppermute(coef, "node", [(i, i ^ shift) for i in range(nodes)])
-        other = moved if shift == 1 else other + moved
+    )(column_blocks, *listed, hamiltonian)
 
     first = call(
         sweep_kernel,
@@ -210,7 +209,12 @@
         moved=rows * wide * 4 + 16 * rows * vecs,
         name="sweep",
     )(high, low, start_basis, start_core, start_chip)
+    first, coef = lax.optimization_barrier((first, coef))
     first_core, first_chip = halo(first)
+    other = coef
+    for shift in range(1, nodes):
+        moved = lax.ppermute(coef, "node", [(i, i ^ shift) for i in range(nodes)])
+        other = moved if shift == 1 else other + moved
 
     half = vecs // 2
     part = jax.ShapeDtypeStruct((half + SUBLANES, half), f32)

time: 41.7 us -> 39.6 us (0.950)
  waiting for transfers between devices: 20.1 us -> 16.3 us
  starting transfers between devices: 11.9 us -> 15.6 us
  local copies, waits for them, and re-layouts: 4.53 us -> 2.52 us
    ppermute x3, starting transfers between devices: 0.43 us -> 3.65 us  [on_device(): lax.ppermute(total, 'row', [(i, i ^ step) for i in range(devices)])]
    ppermute x3, waiting for transfers between devices: 13.8 us -> 11.3 us  [on_device(): lax.ppermute(total, 'row', [(i, i ^ step) for i in range(devices)])]
    another operation x2 -> x0, local copies, waits for them, and re-layouts: 1.92 us -> none  [the longest x1 1.92 us: on_device(): coef = jnp.broadcast_to(jnp.stack(listed)[:, None], (SUBLANES, 128))]
    ppermute x2, waiting for transfers between devices: 1.72 us -> 0.77 us  [halo(): chip = lax.ppermute(block, 'row', chip_pairs)]
    broadcast_in_dim x0 -> x2, other arithmetic: none -> 0.74 us  [on_device(): (active * (weight_re * power_re - weight_im * power_im))[None, :]]
    reduce_sum x1 -> x0, other arithmetic: 0.65 us -> none  [on_device(): jnp.sum(active * (weight_re * power_re - weight_im * power_im))]
    unnamed x16 -> x12, local copies, waits for them, and re-layouts: 2.54 us -> 2.52 us
  transfers between devices with their start and end apart: 10 -> 10, of which waited for: 7 -> 8; matrix products, arithmetic and copies ran while one was open for 6% -> 2% of each run, Pallas kernels for 2% -> 2%
where the time goes in v2:
time: 39.6 us; the launch traced here: 39.4 us
  waiting for transfers between devices  16.3 us (41%)
  starting transfers between devices  15.6 us (39%)
  Pallas kernels  4.11 us (10%)
  local copies, waits for them, and re-layouts  2.52 us (6%)
  other arithmetic  0.78 us (2%)
    ppermute x3, waiting for transfers between devices, on_device(): lax.ppermute(total, 'row', [(i, i ^ step) for i in range(devices)])  11.3 us
    ppermute x2, starting transfers between devices, halo(): chip = lax.ppermute(block, 'row', chip_pairs)  9.94 us
    ppermute x3, starting transfers between devices, on_device(): lax.ppermute(total, 'row', [(i, i ^ step) for i in range(devices)])  3.65 us
    unnamed x12, local copies, waits for them, and re-layouts  2.52 us
    ppermute x1, waiting for transfers between devices, on_device(): moved = lax.ppermute(coef, 'node', [(i, i ^ shift) for i in range(nodes)])  2.11 us
    pallas_call x1, Pallas kernels, on_device(): call(functools.partial(finish_kernel, row_scale), jax.ShapeDtypeStruct((r...  1.88 us
    ppermute x1, starting transfers between devices, on_device(): moved = lax.ppermute(coef, 'node', [(i, i ^ shift) for i in range(nodes)])  1.49 us
    ppermute x1, waiting for transfers between devices, on_device(): theirs = lax.ppermute(total, 'row', core_pairs)  1.25 us
  transfers between devices with their start and end apart: 10, of which 8 were waited for; matrix products, arithmetic and copies ran while one was open for 2% of the time, Pallas kernels for 2%

profile of v2, /device:TPU:0, one launch (start us, length us, event | category | flops | bytes accessed | tf_op | source)
XLA Modules:
  0.0 39.4 jit_solution(4882520816543134757)
XLA Ops:
  0.0 5.4 %collective-permute-start.1 = (f32[256,256]{1,0:T(8,128)}, f32[256,256]{1,0:T(8,128)S(1)}, u32[]{:S(2)}, u32[]{:S(2)}) collective-permute-start(f32[256,256]{1,0:T(8,128)} %start_ref.1), channel_id=1, source_target_pairs={{0,15},{1,2},{2,1},{3,4},{4,3},{5,6},{6,5},{7,8},{8,7},{9,10},{10,... | collective-permute-start | bytes 786440 | tf_op jit(solution)/shard_map/ppermute | solution.py:170
  5.4 0.0 collective-permute-start
  5.4 0.7 %fusion.2 = (f32[1,3]{1,0:T(1,128)S(1)}, f32[3]{0:T(128)S(1)}, f32[3]{0:T(128)S(1)}) fusion(s32[3]{0:T(128)} %param.15, f32[3]{0:T(128)} %param.14, f32[3]{0:T(128)} %param.13, f32[3]{0:T(128)} %param.11, f32[3]{0:T(128)} %param.12), kind=kLoop, calls=%fused_computation.5 | loop fusion | flops 66 | bytes 96 | tf_op jit(solution)/shard_map/broadcast_in_dim | solution.py:181
  6.2 0.0 copy-start.3
  6.2 0.0 copy-start.4
  6.2 0.0 copy-start.5
  6.2 0.6 %copy-done.3 = s32[3]{0:T(128)S(1)} copy-done((s32[3]{0:T(128)S(1)}, s32[3]{0:T(128)}, u32[]{:S(2)}) %copy-start.3) | copy-done | bytes 36
  6.8 0.0 copy-done.4
  6.9 0.0 copy-done.5
  6.9 0.0 copy-start.2
  6.9 0.7 %copy-done.2 = s32[2,7]{1,0:T(2,128)S(1)} copy-done((s32[2,7]{1,0:T(2,128)S(1)}, s32[2,7]{1,0:T(2,128)}, u32[]{:S(2)}) %copy-start.2) | copy-done | bytes 80
  7.6 0.0 copy-start.1
  7.6 1.2 %copy-done.1 = f32[2,7,128,128]{3,2,1,0:T(8,128)S(1)} copy-done((f32[2,7,128,128]{3,2,1,0:T(8,128)S(1)}, f32[2,7,128,128]{3,2,1,0:T(8,128)}, u32[]{:S(2)}) %copy-start.1) | copy-done | bytes 917528
  8.7 0.0 copy-start
  8.7 0.9 %prepare.1 = (bf16[256,768]{1,0:T(8,128)(2,1)S(1)}, bf16[256,768]{1,0:T(8,128)(2,1)S(1)}, s32[8,128]{1,0:T(8,128)S(1)}, f32[8,128]{1,0:T(8,128)S(1)}) custom-call(s32[2,7]{1,0:T(2,128)S(1)} %copy-done.2, f32[1,3]{1,0:T(1,128)S(1)} %get-tuple-element.27.refs_0_, f32[1,3]{1,0:T(1,128)S(1)} %get-tuple-element.26.refs_1_, f32[1,3]{1,0:T(1,128)S(1)} %get-tuple-element.23.refs_2_, ...), custom_call_target="tpu_custom_call" | custom-call | flops 917504 | bytes 2490368 | tf_op jit(solution)/shard_map/prepare/pallas_call | solution.py:188
  9.6 0.2 collective-permute-done.1.chip_ref
  9.8 0.0 collective-permute-done.core_ref
  9.8 0.0 copy-done
  9.8 0.5 %sweep.1.own_ref = f32[256,256]{1,0:T(8,128)S(1)} custom-call(bf16[256,768]{1,0:T(8,128)(2,1)S(1)} %get-tuple-element.14.high_ref, bf16[256,768]{1,0:T(8,128)(2,1)S(1)} %get-tuple-element.15.low_ref, f32[256,256]{1,0:T(8,128)S(1)} %copy-done, f32[256,256]{1,0:T(8,128)S(1)} %collective-permute-done.core_ref, f32[256,256]{1,0:T(8,128)S(1)} %collective-permute-done.1.chip_ref), custom_call_target="tpu_custom_call" | custom-call | flops 301989888 | bytes 1835008 | tf_op jit(solution)/shard_map/sweep/pallas_call | solution.py:204
  10.3 4.5 %collective-permute-start.3 = (f32[256,256]{1,0:T(8,128)S(1)}, f32[256,256]{1,0:T(8,128)S(1)}, u32[]{:S(2)}, u32[]{:S(2)}) collective-permute-start(f32[256,256]{1,0:T(8,128)S(1)} %sweep.1.own_ref), channel_id=1, source_target_pairs={{0,15},{1,2},{2,1},{3,4},{4,3},{5,6},{6,5},{7,8},{8,7},{9,10},{10,... | collective-permute-start | bytes 786440 | tf_op jit(solution)/shard_map/ppermute | solution.py:170
  14.8 0.0 collective-permute-start.2
  14.8 1.5 %collective-permute-start.4 = (f32[8,128]{1,0:T(8,128)S(1)}, f32[8,128]{1,0:T(8,128)S(1)}, u32[]{:S(2)}, u32[]{:S(2)}) collective-permute-start(f32[8,128]{1,0:T(8,128)S(1)} %get-tuple-element.18.coef_ref), channel_id=1, source_target_pairs={{0,16},{16,0},{1,17},{17,1},{2,18},{18,2},{3,19},{19,3},{4,20},{20... | collective-permute-start | bytes 12296 | tf_op jit(solution)/shard_map/ppermute | solution.py:216
  16.3 2.1 %collective-permute-done.4.other_ref = f32[8,128]{1,0:T(8,128)S(1)} collective-permute-done((f32[8,128]{1,0:T(8,128)S(1)}, f32[8,128]{1,0:T(8,128)S(1)}, u32[]{:S(2)}, u32[]{:S(2)}) %collective-permute-start.4) | collective-permute-done | bytes 4128 | tf_op jit(solution)/shard_map/ppermute | solution.py:216
  18.4 0.6 %collective-permute-done.3.chip_ref = f32[256,256]{1,0:T(8,128)S(1)} collective-permute-done((f32[256,256]{1,0:T(8,128)S(1)}, f32[256,256]{1,0:T(8,128)S(1)}, u32[]{:S(2)}, u32[]{:S(2)}) %collective-permute-start.3) | collective-permute-done | bytes 262176 | tf_op jit(solution)/shard_map/ppermute | solution.py:170
  19.0 0.0 collective-permute-done.2.core_ref
  19.0 0.9 %gram.1 = (f32[256,256]{1,0:T(8,128)S(1)}, f32[136,128]{1,0:T(8,128)S(1)}, f32[136,128]{1,0:T(8,128)S(1)}) custom-call(bf16[256,768]{1,0:T(8,128)(2,1)S(1)} %get-tuple-element.14.high_ref, bf16[256,768]{1,0:T(8,128)(2,1)S(1)} %get-tuple-element.15.low_ref, f32[256,256]{1,0:T(8,128)S(1)} %sweep.1.own_ref, f32[256,256]{1,0:T(8,128)S(1)} %collective-permute-done.2.core_ref, ...), custom_call_target="tpu_custom_call" | custom-call | flops 369098752 | bytes 2097152 | tf_op jit(solution)/shard_map/gram/pallas_call | solution.py:221
  19.9 0.4 %collective-permute-start.5 = (f32[136,128]{1,0:T(8,128)S(1)}, f32[136,128]{1,0:T(8,128)S(1)}, u32[]{:S(2)}, u32[]{:S(2)}) collective-permute-start(f32[136,128]{1,0:T(8,128)S(1)} %get-tuple-element.22), channel_id=1, source_target_pairs={{0,1},{1,0},{2,3},{3,2},{4,5},{5,4},{6,7},{7,6},{8,9},{9,8},{10,11... | collective-permute-start | bytes 208904 | tf_op jit(solution)/shard_map/ppermute | solution.py:230
  20.3 0.9 %collective-permute-done.5 = f32[136,128]{1,0:T(8,128)S(1)} collective-permute-done((f32[136,128]{1,0:T(8,128)S(1)}, f32[136,128]{1,0:T(8,128)S(1)}, u32[]{:S(2)}, u32[]{:S(2)}) %collective-permute-start.5) | collective-permute-done | bytes 69664 | tf_op jit(solution)/shard_map/ppermute | solution.py:230
  21.2 1.1 %collective-permute-start.6 = (f32[136,128]{1,0:T(8,128)S(1)}, f32[136,128]{1,0:T(8,128)S(1)}, u32[]{:S(2)}, u32[]{:S(2)}) collective-permute-start(f32[136,128]{1,0:T(8,128)S(1)} %add.24), channel_id=1, source_target_pairs={{0,2},{1,3},{2,0},{3,1},{4,6},{5,7},{6,4},{7,5},{8,10},{9,11},{10,... | collective-permute-start | bytes 208904 | tf_op jit(solution)/shard_map/ppermute | solution.py:233
  22.4 3.4 %collective-permute-done.6 = f32[136,128]{1,0:T(8,128)S(1)} collective-permute-done((f32[136,128]{1,0:T(8,128)S(1)}, f32[136,128]{1,0:T(8,128)S(1)}, u32[]{:S(2)}, u32[]{:S(2)}) %collective-permute-start.6) | collective-permute-done | bytes 69664 | tf_op jit(solution)/shard_map/ppermute | solution.py:233
  25.8 0.8 %collective-permute-start.7 = (f32[136,128]{1,0:T(8,128)S(1)}, f32[136,128]{1,0:T(8,128)S(1)}, u32[]{:S(2)}, u32[]{:S(2)}) collective-permute-start(f32[136,128]{1,0:T(8,128)S(1)} %add.25), channel_id=1, source_target_pairs={{0,4},{1,5},{2,6},{3,7},{4,0},{5,1},{6,2},{7,3},{8,12},{9,13},{10,... | collective-permute-start | bytes 208904 | tf_op jit(solution)/shard_map/ppermute | solution.py:233
  26.5 3.6 %collective-permute-done.7 = f32[136,128]{1,0:T(8,128)S(1)} collective-permute-done((f32[136,128]{1,0:T(8,128)S(1)}, f32[136,128]{1,0:T(8,128)S(1)}, u32[]{:S(2)}, u32[]{:S(2)}) %collective-permute-start.7) | collective-permute-done | bytes 69664 | tf_op jit(solution)/shard_map/ppermute | solution.py:233
  30.2 1.8 %collective-permute-start.8 = (f32[136,128]{1,0:T(8,128)S(1)}, f32[136,128]{1,0:T(8,128)S(1)}, u32[]{:S(2)}, u32[]{:S(2)}) collective-permute-start(f32[136,128]{1,0:T(8,128)S(1)} %add.26), channel_id=1, source_target_pairs={{0,8},{1,9},{2,10},{3,11},{4,12},{5,13},{6,14},{7,15},{8,0},{9,1},... | collective-permute-start | bytes 208904 | tf_op jit(solution)/shard_map/ppermute | solution.py:233
  31.9 4.2 %collective-permute-done.8 = f32[136,128]{1,0:T(8,128)S(1)} collective-permute-done((f32[136,128]{1,0:T(8,128)S(1)}, f32[136,128]{1,0:T(8,128)S(1)}, u32[]{:S(2)}, u32[]{:S(2)}) %collective-permute-start.8) | collective-permute-done | bytes 69664 | tf_op jit(solution)/shard_map/ppermute | solution.py:233
  36.2 0.1 collective-permute-start.9
  36.3 1.2 %collective-permute-done.9.theirs_ref = f32[136,128]{1,0:T(8,128)S(1)} collective-permute-done((f32[136,128]{1,0:T(8,128)S(1)}, f32[136,128]{1,0:T(8,128)S(1)}, u32[]{:S(2)}, u32[]{:S(2)}) %collective-permute-start.9) | collective-permute-done | bytes 69664 | tf_op jit(solution)/shard_map/ppermute | solution.py:235
  37.5 1.9 %finish.1 = f32[256,256]{1,0:T(8,128)} custom-call(f32[256,256]{1,0:T(8,128)S(1)} %get-tuple-element.20.filtered_ref, f32[136,128]{1,0:T(8,128)S(1)} %add.27.mine_ref, f32[136,128]{1,0:T(8,128)S(1)} %collective-permute-done.9.theirs_ref, s32[8,128]{1,0:T(8,128)S(1)} %get-tuple-element.19.odd_ref), custom_call_target="tpu_custom_call" | custom-call | flops 301989888 | bytes 786432 | tf_op jit(solution)/shard_map/finish/pallas_call | solution.py:237
  (5 shorter events, 0.0 us)
Async XLA Ops:
  0.0 9.8 %collective-permute-start.1 = (f32[256,256]{1,0:T(8,128)}, f32[256,256]{1,0:T(8,128)S(1)}, u32[]{:S(2)}, u32[]{:S(2)}) collective-permute-start(f32[256,256]{1,0:T(8,128)} %start_ref.1), channel_id=1, source_target_pairs={{0,15},{1,2},{2,1},{3,4},{4,3},{5,6},{6,5},{7,8},{8,7},{9,10},{10,... | collective-permute-start | bytes 786440 | tf_op jit(solution)/shard_map/ppermute | solution.py:170
  5.4 4.4 %collective-permute-start = (f32[256,256]{1,0:T(8,128)}, f32[256,256]{1,0:T(8,128)S(1)}, u32[]{:S(2)}, u32[]{:S(2)}) collective-permute-start(f32[256,256]{1,0:T(8,128)} %start_ref.1), channel_id=1, source_target_pairs={{0,1},{1,0},{2,3},{3,2},{4,5},{5,4},{6,7},{7,6},{8,9},{9,8},{10,11... | collective-permute-start | bytes 786440 | tf_op jit(solution)/shard_map/ppermute | solution.py:171
  6.2 0.7 %copy-start.3 = (s32[3]{0:T(128)S(1)}, s32[3]{0:T(128)}, u32[]{:S(2)}) copy-start(s32[3]{0:T(128)} %param.15) | copy-start | bytes 40
  6.2 0.7 %copy-start.4 = (f32[3]{0:T(128)S(1)}, f32[3]{0:T(128)}, u32[]{:S(2)}) copy-start(f32[3]{0:T(128)} %param.14) | copy-start | bytes 40
  6.2 0.7 %copy-start.5 = (f32[3]{0:T(128)S(1)}, f32[3]{0:T(128)}, u32[]{:S(2)}) copy-start(f32[3]{0:T(128)} %param.13) | copy-start | bytes 40
  6.9 0.7 %copy-start.2 = (s32[2,7]{1,0:T(2,128)S(1)}, s32[2,7]{1,0:T(2,128)}, u32[]{:S(2)}) copy-start(s32[2,7]{1,0:T(2,128)} %cols_ref.1) | copy-start | bytes 172
  7.6 1.2 %copy-start.1 = (f32[2,7,128,128]{3,2,1,0:T(8,128)S(1)}, f32[2,7,128,128]{3,2,1,0:T(8,128)}, u32[]{:S(2)}) copy-start(f32[2,7,128,128]{3,2,1,0:T(8,128)} %refs_3_.1) | copy-start | bytes 2752516
  8.7 1.1 %copy-start = (f32[256,256]{1,0:T(8,128)S(1)}, f32[256,256]{1,0:T(8,128)}, u32[]{:S(2)}) copy-start(f32[256,256]{1,0:T(8,128)} %start_ref.1) | copy-start | bytes 786436
  10.3 8.7 %collective-permute-start.3 = (f32[256,256]{1,0:T(8,128)S(1)}, f32[256,256]{1,0:T(8,128)S(1)}, u32[]{:S(2)}, u32[]{:S(2)}) collective-permute-start(f32[256,256]{1,0:T(8,128)S(1)} %sweep.1.own_ref), channel_id=1, source_target_pairs={{0,15},{1,2},{2,1},{3,4},{4,3},{5,6},{6,5},{7,8},{8,7},{9,10},{10,... | collective-permute-start | bytes 786440 | tf_op jit(solution)/shard_map/ppermute | solution.py:170
  14.8 4.2 %collective-permute-start.2 = (f32[256,256]{1,0:T(8,128)S(1)}, f32[256,256]{1,0:T(8,128)S(1)}, u32[]{:S(2)}, u32[]{:S(2)}) collective-permute-start(f32[256,256]{1,0:T(8,128)S(1)} %sweep.1.own_ref), channel_id=1, source_target_pairs={{0,1},{1,0},{2,3},{3,2},{4,5},{5,4},{6,7},{7,6},{8,9},{9,8},{10,11... | collective-permute-start | bytes 786440 | tf_op jit(solution)/shard_map/ppermute | solution.py:171
  14.8 3.6 %collective-permute-start.4 = (f32[8,128]{1,0:T(8,128)S(1)}, f32[8,128]{1,0:T(8,128)S(1)}, u32[]{:S(2)}, u32[]{:S(2)}) collective-permute-start(f32[8,128]{1,0:T(8,128)S(1)} %get-tuple-element.18.coef_ref), channel_id=1, source_target_pairs={{0,16},{16,0},{1,17},{17,1},{2,18},{18,2},{3,19},{19,3},{4,20},{20... | collective-permute-start | bytes 12296 | tf_op jit(solution)/shard_map/ppermute | solution.py:216
  19.9 1.4 %collective-permute-start.5 = (f32[136,128]{1,0:T(8,128)S(1)}, f32[136,128]{1,0:T(8,128)S(1)}, u32[]{:S(2)}, u32[]{:S(2)}) collective-permute-start(f32[136,128]{1,0:T(8,128)S(1)} %get-tuple-element.22), channel_id=1, source_target_pairs={{0,1},{1,0},{2,3},{3,2},{4,5},{5,4},{6,7},{7,6},{8,9},{9,8},{10,11... | collective-permute-start | bytes 208904 | tf_op jit(solution)/shard_map/ppermute | solution.py:230
  21.2 4.5 %collective-permute-start.6 = (f32[136,128]{1,0:T(8,128)S(1)}, f32[136,128]{1,0:T(8,128)S(1)}, u32[]{:S(2)}, u32[]{:S(2)}) collective-permute-start(f32[136,128]{1,0:T(8,128)S(1)} %add.24), channel_id=1, source_target_pairs={{0,2},{1,3},{2,0},{3,1},{4,6},{5,7},{6,4},{7,5},{8,10},{9,11},{10,... | collective-permute-start | bytes 208904 | tf_op jit(solution)/shard_map/ppermute | solution.py:233
  25.8 4.4 %collective-permute-start.7 = (f32[136,128]{1,0:T(8,128)S(1)}, f32[136,128]{1,0:T(8,128)S(1)}, u32[]{:S(2)}, u32[]{:S(2)}) collective-permute-start(f32[136,128]{1,0:T(8,128)S(1)} %add.25), channel_id=1, source_target_pairs={{0,4},{1,5},{2,6},{3,7},{4,0},{5,1},{6,2},{7,3},{8,12},{9,13},{10,... | collective-permute-start | bytes 208904 | tf_op jit(solution)/shard_map/ppermute | solution.py:233
  30.2 6.0 %collective-permute-start.8 = (f32[136,128]{1,0:T(8,128)S(1)}, f32[136,128]{1,0:T(8,128)S(1)}, u32[]{:S(2)}, u32[]{:S(2)}) collective-permute-start(f32[136,128]{1,0:T(8,128)S(1)} %add.26), channel_id=1, source_target_pairs={{0,8},{1,9},{2,10},{3,11},{4,12},{5,13},{6,14},{7,15},{8,0},{9,1},... | collective-permute-start | bytes 208904 | tf_op jit(solution)/shard_map/ppermute | solution.py:233
  36.2 1.3 %collective-permute-start.9 = (f32[136,128]{1,0:T(8,128)S(1)}, f32[136,128]{1,0:T(8,128)S(1)}, u32[]{:S(2)}, u32[]{:S(2)}) collective-permute-start(f32[136,128]{1,0:T(8,128)S(1)} %add.27.mine_ref), channel_id=1, source_target_pairs={{0,1},{1,0},{2,3},{3,2},{4,5},{5,4},{6,7},{7,6},{8,9},{9,8},{10,11... | collective-permute-start | bytes 208904 | tf_op jit(solution)/shard_map/ppermute | solution.py:235

commit v3 on v2

--- a/solution.py
+++ b/solution.py
@@ -139,6 +139,13 @@
     out_ref[...] = scale * (Z_POLY[0] * filtered + mm3(f_high, f_low, z_high, z_low))
 
 
+def sum_up(total, moved):
+    total = total + moved[0]
+    if len(moved) == 3:
+        total = total + (moved[1] + moved[2])
+    return total
+
+
 def call(kernel, out_shape, n_in, smem=(), scratch=(), flops=0, moved=0, name=None):
     n_out = len(out_shape) if isinstance(out_shape, (tuple, list)) else 1
     return pl.pallas_call(
@@ -228,10 +235,13 @@
     )(high, low, first, first_core, first_chip, start_basis, coef, other, odd)
 
     total = mine + lax.ppermute(theirs, "row", core_pairs)
-    step = 2
-    while step < devices:
-        total = total + lax.ppermute(total, "row", [(i, i ^ step) for i in range(devices)])
-        step *= 2
+    steps = [1 << bit for bit in range(1, (devices - 1).bit_length())]
+    phases = [[steps[0], steps[1], steps[0] + steps[1]]] if len(steps) > 1 else [steps]
+    for phase in phases + [[step] for step in steps[2:]]:
+        moved = [
+            lax.ppermute(total, "row", [(i, i ^ step) for i in range(devices)]) for step in phase
+        ]
+        total = sum_up(total, moved)
     theirs = lax.ppermute(total, "row", core_pairs)
 
     return call(

time: 39.6 us -> 37 us (0.934)
  waiting for transfers between devices: 16.3 us -> 11.1 us
  starting transfers between devices: 15.6 us -> 18.2 us
    ppermute x3 -> x4, waiting for transfers between devices: 11.3 us -> 6.09 us  [on_device(): lax.ppermute(total, 'row', [(i, i ^ step) for i in range(devices)])]
    ppermute x3 -> x4, starting transfers between devices: 3.65 us -> 6.2 us  [on_device(): lax.ppermute(total, 'row', [(i, i ^ step) for i in range(devices)])]
  transfers between devices with their start and end apart: 10 -> 11, of which waited for: 8 -> 9; matrix products, arithmetic and copies ran while one was open for 2% -> 2% of each run, Pallas kernels for 2% -> 2%
where the time goes in v3:
time: 37 us; the launch traced here: 36.8 us
  starting transfers between devices  18.2 us (49%)
  waiting for transfers between devices  11.1 us (30%)
  Pallas kernels  4.11 us (11%)
  local copies, waits for them, and re-layouts  2.52 us (7%)
  other arithmetic  0.78 us (2%)
    ppermute x2, starting transfers between devices, halo(): chip = lax.ppermute(block, 'row', chip_pairs)  9.94 us
    ppermute x4, starting transfers between devices, on_device(): lax.ppermute(total, 'row', [(i, i ^ step) for i in range(devices)])  6.2 us
    ppermute x4, waiting for transfers between devices, on_device(): lax.ppermute(total, 'row', [(i, i ^ step) for i in range(devices)])  6.09 us
    unnamed x12, local copies, waits for them, and re-layouts  2.52 us
    ppermute x1, waiting for transfers between devices, on_device(): moved = lax.ppermute(coef, 'node', [(i, i ^ shift) for i in range(nodes)])  2.11 us
    pallas_call x1, Pallas kernels, on_device(): call(functools.partial(finish_kernel, row_scale), jax.ShapeDtypeStruct((r...  1.88 us
    ppermute x1, starting transfers between devices, on_device(): moved = lax.ppermute(coef, 'node', [(i, i ^ shift) for i in range(nodes)])  1.49 us
    ppermute x1, waiting for transfers between devices, on_device(): theirs = lax.ppermute(total, 'row', core_pairs)  1.25 us
  transfers between devices with their start and end apart: 11, of which 9 were waited for; matrix products, arithmetic and copies ran while one was open for 2% of the time, Pallas kernels for 2%

profile of v3, /device:TPU:0, one launch (start us, length us, event | category | flops | bytes accessed | tf_op | source)
XLA Modules:
  0.0 36.8 jit_solution(11305141213580036512)
XLA Ops:
  0.0 5.4 %collective-permute-start.1 = (f32[256,256]{1,0:T(8,128)}, f32[256,256]{1,0:T(8,128)S(1)}, u32[]{:S(2)}, u32[]{:S(2)}) collective-permute-start(f32[256,256]{1,0:T(8,128)} %start_ref.1), channel_id=1, source_target_pairs={{0,15},{1,2},{2,1},{3,4},{4,3},{5,6},{6,5},{7,8},{8,7},{9,10},{10,... | collective-permute-start | bytes 786440 | tf_op jit(solution)/shard_map/ppermute | solution.py:177
  5.4 0.0 collective-permute-start
  5.4 0.7 %fusion.2 = (f32[1,3]{1,0:T(1,128)S(1)}, f32[3]{0:T(128)S(1)}, f32[3]{0:T(128)S(1)}) fusion(s32[3]{0:T(128)} %param.15, f32[3]{0:T(128)} %param.14, f32[3]{0:T(128)} %param.13, f32[3]{0:T(128)} %param.11, f32[3]{0:T(128)} %param.12), kind=kLoop, calls=%fused_computation.6 | loop fusion | flops 66 | bytes 96 | tf_op jit(solution)/shard_map/broadcast_in_dim | solution.py:188
  6.2 0.0 copy-start.3
  6.2 0.0 copy-start.4
  6.2 0.0 copy-start.5
  6.2 0.6 %copy-done.3 = s32[3]{0:T(128)S(1)} copy-done((s32[3]{0:T(128)S(1)}, s32[3]{0:T(128)}, u32[]{:S(2)}) %copy-start.3) | copy-done | bytes 36
  6.8 0.0 copy-done.4
  6.9 0.0 copy-done.5
  6.9 0.0 copy-start.2
  6.9 0.7 %copy-done.2 = s32[2,7]{1,0:T(2,128)S(1)} copy-done((s32[2,7]{1,0:T(2,128)S(1)}, s32[2,7]{1,0:T(2,128)}, u32[]{:S(2)}) %copy-start.2) | copy-done | bytes 80
  7.6 0.0 copy-start.1
  7.6 1.2 %copy-done.1 = f32[2,7,128,128]{3,2,1,0:T(8,128)S(1)} copy-done((f32[2,7,128,128]{3,2,1,0:T(8,128)S(1)}, f32[2,7,128,128]{3,2,1,0:T(8,128)}, u32[]{:S(2)}) %copy-start.1) | copy-done | bytes 917528
  8.7 0.0 copy-start
  8.7 0.9 %prepare.1 = (bf16[256,768]{1,0:T(8,128)(2,1)S(1)}, bf16[256,768]{1,0:T(8,128)(2,1)S(1)}, s32[8,128]{1,0:T(8,128)S(1)}, f32[8,128]{1,0:T(8,128)S(1)}) custom-call(s32[2,7]{1,0:T(2,128)S(1)} %copy-done.2, f32[1,3]{1,0:T(1,128)S(1)} %get-tuple-element.27.refs_0_, f32[1,3]{1,0:T(1,128)S(1)} %get-tuple-element.26.refs_1_, f32[1,3]{1,0:T(1,128)S(1)} %get-tuple-element.23.refs_2_, ...), custom_call_target="tpu_custom_call" | custom-call | flops 917504 | bytes 2490368 | tf_op jit(solution)/shard_map/prepare/pallas_call | solution.py:195
  9.6 0.2 collective-permute-done.1.chip_ref
  9.8 0.0 collective-permute-done.core_ref
  9.8 0.0 copy-done
  9.8 0.5 %sweep.1.own_ref = f32[256,256]{1,0:T(8,128)S(1)} custom-call(bf16[256,768]{1,0:T(8,128)(2,1)S(1)} %get-tuple-element.14.high_ref, bf16[256,768]{1,0:T(8,128)(2,1)S(1)} %get-tuple-element.15.low_ref, f32[256,256]{1,0:T(8,128)S(1)} %copy-done, f32[256,256]{1,0:T(8,128)S(1)} %collective-permute-done.core_ref, f32[256,256]{1,0:T(8,128)S(1)} %collective-permute-done.1.chip_ref), custom_call_target="tpu_custom_call" | custom-call | flops 301989888 | bytes 1835008 | tf_op jit(solution)/shard_map/sweep/pallas_call | solution.py:211
  10.3 4.5 %collective-permute-start.3 = (f32[256,256]{1,0:T(8,128)S(1)}, f32[256,256]{1,0:T(8,128)S(1)}, u32[]{:S(2)}, u32[]{:S(2)}) collective-permute-start(f32[256,256]{1,0:T(8,128)S(1)} %sweep.1.own_ref), channel_id=1, source_target_pairs={{0,15},{1,2},{2,1},{3,4},{4,3},{5,6},{6,5},{7,8},{8,7},{9,10},{10,... | collective-permute-start | bytes 786440 | tf_op jit(solution)/shard_map/ppermute | solution.py:177
  14.8 0.0 collective-permute-start.2
  14.8 1.5 %collective-permute-start.4 = (f32[8,128]{1,0:T(8,128)S(1)}, f32[8,128]{1,0:T(8,128)S(1)}, u32[]{:S(2)}, u32[]{:S(2)}) collective-permute-start(f32[8,128]{1,0:T(8,128)S(1)} %get-tuple-element.18.coef_ref), channel_id=1, source_target_pairs={{0,16},{16,0},{1,17},{17,1},{2,18},{18,2},{3,19},{19,3},{4,20},{20... | collective-permute-start | bytes 12296 | tf_op jit(solution)/shard_map/ppermute | solution.py:223
  16.3 2.1 %collective-permute-done.4.other_ref = f32[8,128]{1,0:T(8,128)S(1)} collective-permute-done((f32[8,128]{1,0:T(8,128)S(1)}, f32[8,128]{1,0:T(8,128)S(1)}, u32[]{:S(2)}, u32[]{:S(2)}) %collective-permute-start.4) | collective-permute-done | bytes 4128 | tf_op jit(solution)/shard_map/ppermute | solution.py:223
  18.4 0.6 %collective-permute-done.3.chip_ref = f32[256,256]{1,0:T(8,128)S(1)} collective-permute-done((f32[256,256]{1,0:T(8,128)S(1)}, f32[256,256]{1,0:T(8,128)S(1)}, u32[]{:S(2)}, u32[]{:S(2)}) %collective-permute-start.3) | collective-permute-done | bytes 262176 | tf_op jit(solution)/shard_map/ppermute | solution.py:177
  19.0 0.0 collective-permute-done.2.core_ref
  19.0 0.9 %gram.1 = (f32[256,256]{1,0:T(8,128)S(1)}, f32[136,128]{1,0:T(8,128)S(1)}, f32[136,128]{1,0:T(8,128)S(1)}) custom-call(bf16[256,768]{1,0:T(8,128)(2,1)S(1)} %get-tuple-element.14.high_ref, bf16[256,768]{1,0:T(8,128)(2,1)S(1)} %get-tuple-element.15.low_ref, f32[256,256]{1,0:T(8,128)S(1)} %sweep.1.own_ref, f32[256,256]{1,0:T(8,128)S(1)} %collective-permute-done.2.core_ref, ...), custom_call_target="tpu_custom_call" | custom-call | flops 369098752 | bytes 2097152 | tf_op jit(solution)/shard_map/gram/pallas_call | solution.py:228
  19.9 0.4 %collective-permute-start.5 = (f32[136,128]{1,0:T(8,128)S(1)}, f32[136,128]{1,0:T(8,128)S(1)}, u32[]{:S(2)}, u32[]{:S(2)}) collective-permute-start(f32[136,128]{1,0:T(8,128)S(1)} %get-tuple-element.22), channel_id=1, source_target_pairs={{0,1},{1,0},{2,3},{3,2},{4,5},{5,4},{6,7},{7,6},{8,9},{9,8},{10,11... | collective-permute-start | bytes 208904 | tf_op jit(solution)/shard_map/ppermute | solution.py:237
  20.3 0.9 %collective-permute-done.5 = f32[136,128]{1,0:T(8,128)S(1)} collective-permute-done((f32[136,128]{1,0:T(8,128)S(1)}, f32[136,128]{1,0:T(8,128)S(1)}, u32[]{:S(2)}, u32[]{:S(2)}) %collective-permute-start.5) | collective-permute-done | bytes 69664 | tf_op jit(solution)/shard_map/ppermute | solution.py:237
  21.2 2.1 %collective-permute-start.8 = (f32[136,128]{1,0:T(8,128)S(1)}, f32[136,128]{1,0:T(8,128)S(1)}, u32[]{:S(2)}, u32[]{:S(2)}) collective-permute-start(f32[136,128]{1,0:T(8,128)S(1)} %add.27), channel_id=1, source_target_pairs={{0,6},{1,7},{2,4},{3,5},{4,2},{5,3},{6,0},{7,1},{8,14},{9,15},{10,... | collective-permute-start | bytes 208904 | tf_op jit(solution)/shard_map/ppermute | solution.py:242
  23.4 0.5 %collective-permute-start.7 = (f32[136,128]{1,0:T(8,128)S(1)}, f32[136,128]{1,0:T(8,128)S(1)}, u32[]{:S(2)}, u32[]{:S(2)}) collective-permute-start(f32[136,128]{1,0:T(8,128)S(1)} %add.27), channel_id=1, source_target_pairs={{0,4},{1,5},{2,6},{3,7},{4,0},{5,1},{6,2},{7,3},{8,12},{9,13},{10,... | collective-permute-start | bytes 208904 | tf_op jit(solution)/shard_map/ppermute | solution.py:242
  23.8 1.0 %collective-permute-start.6 = (f32[136,128]{1,0:T(8,128)S(1)}, f32[136,128]{1,0:T(8,128)S(1)}, u32[]{:S(2)}, u32[]{:S(2)}) collective-permute-start(f32[136,128]{1,0:T(8,128)S(1)} %add.27), channel_id=1, source_target_pairs={{0,2},{1,3},{2,0},{3,1},{4,6},{5,7},{6,4},{7,5},{8,10},{9,11},{10,... | collective-permute-start | bytes 208904 | tf_op jit(solution)/shard_map/ppermute | solution.py:242
  24.8 2.4 %collective-permute-done.8 = f32[136,128]{1,0:T(8,128)S(1)} collective-permute-done((f32[136,128]{1,0:T(8,128)S(1)}, f32[136,128]{1,0:T(8,128)S(1)}, u32[]{:S(2)}, u32[]{:S(2)}) %collective-permute-start.8) | collective-permute-done | bytes 69664 | tf_op jit(solution)/shard_map/ppermute | solution.py:242
  27.2 0.5 %collective-permute-done.7 = f32[136,128]{1,0:T(8,128)S(1)} collective-permute-done((f32[136,128]{1,0:T(8,128)S(1)}, f32[136,128]{1,0:T(8,128)S(1)}, u32[]{:S(2)}, u32[]{:S(2)}) %collective-permute-start.7) | collective-permute-done | bytes 69664 | tf_op jit(solution)/shard_map/ppermute | solution.py:242
  27.7 0.5 %collective-permute-done.6 = f32[136,128]{1,0:T(8,128)S(1)} collective-permute-done((f32[136,128]{1,0:T(8,128)S(1)}, f32[136,128]{1,0:T(8,128)S(1)}, u32[]{:S(2)}, u32[]{:S(2)}) %collective-permute-start.6) | collective-permute-done | bytes 69664 | tf_op jit(solution)/shard_map/ppermute | solution.py:242
  28.2 2.6 %collective-permute-start.9 = (f32[136,128]{1,0:T(8,128)S(1)}, f32[136,128]{1,0:T(8,128)S(1)}, u32[]{:S(2)}, u32[]{:S(2)}) collective-permute-start(f32[136,128]{1,0:T(8,128)S(1)} %add_add_fusion), channel_id=1, source_target_pairs={{0,8},{1,9},{2,10},{3,11},{4,12},{5,13},{6,14},{7,15},{8,0},{9,1},... | collective-permute-start | bytes 208904 | tf_op jit(solution)/shard_map/ppermute | solution.py:242
  30.8 2.8 %collective-permute-done.9 = f32[136,128]{1,0:T(8,128)S(1)} collective-permute-done((f32[136,128]{1,0:T(8,128)S(1)}, f32[136,128]{1,0:T(8,128)S(1)}, u32[]{:S(2)}, u32[]{:S(2)}) %collective-permute-start.9) | collective-permute-done | bytes 69664 | tf_op jit(solution)/shard_map/ppermute | solution.py:242
  33.6 0.1 collective-permute-start.10
  33.7 1.2 %collective-permute-done.10.theirs_ref = f32[136,128]{1,0:T(8,128)S(1)} collective-permute-done((f32[136,128]{1,0:T(8,128)S(1)}, f32[136,128]{1,0:T(8,128)S(1)}, u32[]{:S(2)}, u32[]{:S(2)}) %collective-permute-start.10) | collective-permute-done | bytes 69664 | tf_op jit(solution)/shard_map/ppermute | solution.py:245
  34.9 1.9 %finish.1 = f32[256,256]{1,0:T(8,128)} custom-call(f32[256,256]{1,0:T(8,128)S(1)} %get-tuple-element.20.filtered_ref, f32[136,128]{1,0:T(8,128)S(1)} %add.31.mine_ref, f32[136,128]{1,0:T(8,128)S(1)} %collective-permute-done.10.theirs_ref, s32[8,128]{1,0:T(8,128)S(1)} %get-tuple-element.19.odd_ref), custom_call_target="tpu_custom_call" | custom-call | flops 301989888 | bytes 786432 | tf_op jit(solution)/shard_map/finish/pallas_call | solution.py:247
  (4 shorter events, 0.0 us)
Async XLA Ops:
  0.0 9.8 %collective-permute-start.1 = (f32[256,256]{1,0:T(8,128)}, f32[256,256]{1,0:T(8,128)S(1)}, u32[]{:S(2)}, u32[]{:S(2)}) collective-permute-start(f32[256,256]{1,0:T(8,128)} %start_ref.1), channel_id=1, source_target_pairs={{0,15},{1,2},{2,1},{3,4},{4,3},{5,6},{6,5},{7,8},{8,7},{9,10},{10,... | collective-permute-start | bytes 786440 | tf_op jit(solution)/shard_map/ppermute | solution.py:177
  5.4 4.4 %collective-permute-start = (f32[256,256]{1,0:T(8,128)}, f32[256,256]{1,0:T(8,128)S(1)}, u32[]{:S(2)}, u32[]{:S(2)}) collective-permute-start(f32[256,256]{1,0:T(8,128)} %start_ref.1), channel_id=1, source_target_pairs={{0,1},{1,0},{2,3},{3,2},{4,5},{5,4},{6,7},{7,6},{8,9},{9,8},{10,11... | collective-permute-start | bytes 786440 | tf_op jit(solution)/shard_map/ppermute | solution.py:178
  6.2 0.7 %copy-start.3 = (s32[3]{0:T(128)S(1)}, s32[3]{0:T(128)}, u32[]{:S(2)}) copy-start(s32[3]{0:T(128)} %param.15) | copy-start | bytes 40
  6.2 0.7 %copy-start.4 = (f32[3]{0:T(128)S(1)}, f32[3]{0:T(128)}, u32[]{:S(2)}) copy-start(f32[3]{0:T(128)} %param.14) | copy-start | bytes 40
  6.2 0.7 %copy-start.5 = (f32[3]{0:T(128)S(1)}, f32[3]{0:T(128)}, u32[]{:S(2)}) copy-start(f32[3]{0:T(128)} %param.13) | copy-start | bytes 40
  6.9 0.7 %copy-start.2 = (s32[2,7]{1,0:T(2,128)S(1)}, s32[2,7]{1,0:T(2,128)}, u32[]{:S(2)}) copy-start(s32[2,7]{1,0:T(2,128)} %cols_ref.1) | copy-start | bytes 172
  7.6 1.2 %copy-start.1 = (f32[2,7,128,128]{3,2,1,0:T(8,128)S(1)}, f32[2,7,128,128]{3,2,1,0:T(8,128)}, u32[]{:S(2)}) copy-start(f32[2,7,128,128]{3,2,1,0:T(8,128)} %refs_3_.1) | copy-start | bytes 2752516
  8.7 1.1 %copy-start = (f32[256,256]{1,0:T(8,128)S(1)}, f32[256,256]{1,0:T(8,128)}, u32[]{:S(2)}) copy-start(f32[256,256]{1,0:T(8,128)} %start_ref.1) | copy-start | bytes 786436
  10.3 8.7 %collective-permute-start.3 = (f32[256,256]{1,0:T(8,128)S(1)}, f32[256,256]{1,0:T(8,128)S(1)}, u32[]{:S(2)}, u32[]{:S(2)}) collective-permute-start(f32[256,256]{1,0:T(8,128)S(1)} %sweep.1.own_ref), channel_id=1, source_target_pairs={{0,15},{1,2},{2,1},{3,4},{4,3},{5,6},{6,5},{7,8},{8,7},{9,10},{10,... | collective-permute-start | bytes 786440 | tf_op jit(solution)/shard_map/ppermute | solution.py:177
  14.8 4.2 %collective-permute-start.2 = (f32[256,256]{1,0:T(8,128)S(1)}, f32[256,256]{1,0:T(8,128)S(1)}, u32[]{:S(2)}, u32[]{:S(2)}) collective-permute-start(f32[256,256]{1,0:T(8,128)S(1)} %sweep.1.own_ref), channel_id=1, source_target_pairs={{0,1},{1,0},{2,3},{3,2},{4,5},{5,4},{6,7},{7,6},{8,9},{9,8},{10,11... | collective-permute-start | bytes 786440 | tf_op jit(solution)/shard_map/ppermute | solution.py:178
  14.8 3.6 %collective-permute-start.4 = (f32[8,128]{1,0:T(8,128)S(1)}, f32[8,128]{1,0:T(8,128)S(1)}, u32[]{:S(2)}, u32[]{:S(2)}) collective-permute-start(f32[8,128]{1,0:T(8,128)S(1)} %get-tuple-element.18.coef_ref), channel_id=1, source_target_pairs={{0,16},{16,0},{1,17},{17,1},{2,18},{18,2},{3,19},{19,3},{4,20},{20... | collective-permute-start | bytes 12296 | tf_op jit(solution)/shard_map/ppermute | solution.py:223
  19.9 1.4 %collective-permute-start.5 = (f32[136,128]{1,0:T(8,128)S(1)}, f32[136,128]{1,0:T(8,128)S(1)}, u32[]{:S(2)}, u32[]{:S(2)}) collective-permute-start(f32[136,128]{1,0:T(8,128)S(1)} %get-tuple-element.22), channel_id=1, source_target_pairs={{0,1},{1,0},{2,3},{3,2},{4,5},{5,4},{6,7},{7,6},{8,9},{9,8},{10,11... | collective-permute-start | bytes 208904 | tf_op jit(solution)/shard_map/ppermute | solution.py:237
  21.2 6.0 %collective-permute-start.8 = (f32[136,128]{1,0:T(8,128)S(1)}, f32[136,128]{1,0:T(8,128)S(1)}, u32[]{:S(2)}, u32[]{:S(2)}) collective-permute-start(f32[136,128]{1,0:T(8,128)S(1)} %add.27), channel_id=1, source_target_pairs={{0,6},{1,7},{2,4},{3,5},{4,2},{5,3},{6,0},{7,1},{8,14},{9,15},{10,... | collective-permute-start | bytes 208904 | tf_op jit(solution)/shard_map/ppermute | solution.py:242
  23.4 4.3 %collective-permute-start.7 = (f32[136,128]{1,0:T(8,128)S(1)}, f32[136,128]{1,0:T(8,128)S(1)}, u32[]{:S(2)}, u32[]{:S(2)}) collective-permute-start(f32[136,128]{1,0:T(8,128)S(1)} %add.27), channel_id=1, source_target_pairs={{0,4},{1,5},{2,6},{3,7},{4,0},{5,1},{6,2},{7,3},{8,12},{9,13},{10,... | collective-permute-start | bytes 208904 | tf_op jit(solution)/shard_map/ppermute | solution.py:242
  23.8 4.3 %collective-permute-start.6 = (f32[136,128]{1,0:T(8,128)S(1)}, f32[136,128]{1,0:T(8,128)S(1)}, u32[]{:S(2)}, u32[]{:S(2)}) collective-permute-start(f32[136,128]{1,0:T(8,128)S(1)} %add.27), channel_id=1, source_target_pairs={{0,2},{1,3},{2,0},{3,1},{4,6},{5,7},{6,4},{7,5},{8,10},{9,11},{10,... | collective-permute-start | bytes 208904 | tf_op jit(solution)/shard_map/ppermute | solution.py:242
  28.2 5.4 %collective-permute-start.9 = (f32[136,128]{1,0:T(8,128)S(1)}, f32[136,128]{1,0:T(8,128)S(1)}, u32[]{:S(2)}, u32[]{:S(2)}) collective-permute-start(f32[136,128]{1,0:T(8,128)S(1)} %add_add_fusion), channel_id=1, source_target_pairs={{0,8},{1,9},{2,10},{3,11},{4,12},{5,13},{6,14},{7,15},{8,0},{9,1},... | collective-permute-start | bytes 208904 | tf_op jit(solution)/shard_map/ppermute | solution.py:242
  33.6 1.3 %collective-permute-start.10 = (f32[136,128]{1,0:T(8,128)S(1)}, f32[136,128]{1,0:T(8,128)S(1)}, u32[]{:S(2)}, u32[]{:S(2)}) collective-permute-start(f32[136,128]{1,0:T(8,128)S(1)} %add.31.mine_ref), channel_id=1, source_target_pairs={{0,1},{1,0},{2,3},{3,2},{4,5},{5,4},{6,7},{7,6},{8,9},{9,8},{10,11... | collective-permute-start | bytes 208904 | tf_op jit(solution)/shard_map/ppermute | solution.py:245

commit v4 on v3

--- a/solution.py
+++ b/solution.py
@@ -13,6 +13,7 @@
 SUBLANES = 8
 
 VMEM = pl.BlockSpec(memory_space=pltpu.VMEM)
+ANY = pl.BlockSpec(memory_space=pl.ANY)
 SMEM = pl.BlockSpec(memory_space=pltpu.SMEM)
 
 
@@ -62,10 +63,10 @@
             low_ref[rows, lanes] = low
 
 
-def banded(high_ref, low_ref, parts):
+def banded(high_ref, low_ref, first, parts):
     rows = parts[0].shape[0]
     total = None
-    for index, part in enumerate(parts):
+    for index, part in enumerate(parts, first):
         lanes = slice(index * rows, (index + 1) * rows)
         b_high, b_low = split(part[...])
         term = mm3(high_ref[:, lanes], low_ref[:, lanes], b_high, b_low)
@@ -73,15 +74,19 @@
     return total
 
 
+def near_kernel(high_ref, low_ref, own_ref, out_ref):
+    out_ref[...] = banded(high_ref, low_ref, 0, (own_ref,))
+
+
 def sweep_kernel(high_ref, low_ref, own_ref, core_ref, chip_ref, out_ref):
-    out_ref[...] = banded(high_ref, low_ref, (own_ref, core_ref, chip_ref))
+    out_ref[...] = banded(high_ref, low_ref, 0, (own_ref, core_ref, chip_ref))
 
 
 def gram_kernel(
-    high_ref, low_ref, own_ref, core_ref, chip_ref, start_ref, coef_ref, other_ref, odd_ref,
+    high_ref, low_ref, own_ref, near_ref, core_ref, chip_ref, start_ref, coef_ref, other_ref, odd_ref,
     filtered_ref, mine_ref, theirs_ref,
 ):
-    second = banded(high_ref, low_ref, (own_ref, core_ref, chip_ref))
+    second = near_ref[...] + banded(high_ref, low_ref, 1, (core_ref, chip_ref))
     coef = coef_ref[...] + other_ref[...]
     filtered = (
         coef[0:1, 0:1] * start_ref[...] + coef[1:2, 0:1] * own_ref[...] + coef[2:3, 0:1] * second
@@ -104,7 +109,7 @@
     theirs_ref[half:] = diagonal
 
 
-def finish_kernel(row_scale, filtered_ref, mine_ref, theirs_ref, odd_ref, out_ref):
+def finish_kernel(row_scale, filtered_ref, mine_ref, theirs_ref, odd_ref, out_ref, held, sems):
     half = mine_ref.shape[1]
     odd = odd_ref[0:1, 0:1] == 1
     mine, theirs = mine_ref[...], theirs_ref[...]
@@ -124,19 +129,32 @@
         ],
         axis=0,
     )
-    square = jnp.sum(jnp.sum(gram * gram, axis=0, keepdims=True), axis=1, keepdims=True)
+    g_high, g_low = split(gram)
+    gram2 = mm3(g_high, g_low, g_high, g_low)
+    squares = upper * upper + lower * lower + 2.0 * (side * side)
+    square = jnp.sum(jnp.sum(squares, axis=0, keepdims=True), axis=1, keepdims=True)
     norm_value = jnp.sqrt(square + 1e-06)
-    a = gram / norm_value
-    a_high, a_low = split(a)
-    a2 = mm3(a_high, a_low, a_high, a_low)
+    inverse = 1.0 / norm_value
+    a = gram * inverse
+    a2 = (gram2 * inverse) * inverse
     b_high, b_low = split(a2)
     c_high, c_low = split(Z_POLY[3] * a + Z_POLY[4] * a2)
     rest = Z_POLY[1] * a + Z_POLY[2] * a2 + mm3(b_high, b_low, c_high, c_low)
+    scale = row_scale / jnp.sqrt(norm_value)
     z_high, z_low = split(rest)
-    filtered = filtered_ref[...]
-    f_high, f_low = split(filtered)
-    scale = row_scale / jnp.sqrt(norm_value)
-    out_ref[...] = scale * (Z_POLY[0] * filtered + mm3(f_high, f_low, z_high, z_low))
+    pieces = sems.shape[0]
+    rows = out_ref.shape[0] // pieces
+    copies = []
+    for piece in range(pieces):
+        part = pl.ds(piece * rows, rows)
+        filtered = filtered_ref[part, :]
+        f_high, f_low = split(filtered)
+        held[part, :] = scale * (Z_POLY[0] * filtered + mm3(f_high, f_low, z_high, z_low))
+        copy = pltpu.make_async_copy(held.at[part, :], out_ref.at[part, :], sems.at[piece])
+        copy.start()
+        copies.append(copy)
+    for copy in copies:
+        copy.wait()
 
 
 def sum_up(total, moved):
@@ -146,13 +164,13 @@
     return total
 
 
-def call(kernel, out_shape, n_in, smem=(), scratch=(), flops=0, moved=0, name=None):
+def call(kernel, out_shape, n_in, smem=(), out_any=False, scratch=(), flops=0, moved=0, name=None):
     n_out = len(out_shape) if isinstance(out_shape, (tuple, list)) else 1
     return pl.pallas_call(
         kernel,
         out_shape=out_shape,
         in_specs=[SMEM if i in smem else VMEM for i in range(n_in)],
-        out_specs=[VMEM] * n_out if isinstance(out_shape, (tuple, list)) else VMEM,
+        out_specs=[VMEM] * n_out if isinstance(out_shape, (tuple, list)) else ANY if out_any else VMEM,
         scratch_shapes=scratch,
         cost_estimate=pl.CostEstimate(flops=flops, bytes_accessed=moved, transcendentals=0),
         compiler_params=pltpu.CompilerParams(vmem_limit_bytes=24 * 2**20),
@@ -208,13 +226,17 @@
         name="prepare",
     )(column_blocks, *listed, hamiltonian)
 
+    square = jax.ShapeDtypeStruct((rows, vecs), f32)
+
+    def near(own):
+        return call(
+            near_kernel, square, 3,
+            flops=12 * rows * rows * vecs, moved=8 * rows * rows + 12 * rows * vecs, name="near",
+        )(high, low, own)
+
     first = call(
-        sweep_kernel,
-        jax.ShapeDtypeStruct((rows, vecs), f32),
-        5,
-        flops=6 * rows * wide * vecs,
-        moved=rows * wide * 4 + 16 * rows * vecs,
-        name="sweep",
+        sweep_kernel, square, 5,
+        flops=6 * rows * rows * vecs, moved=4 * rows * rows + 12 * rows * vecs, name="sweep",
     )(high, low, start_basis, start_core, start_chip)
     first, coef = lax.optimization_barrier((first, coef))
     first_core, first_chip = halo(first)
@@ -228,11 +250,11 @@
     filtered, mine, theirs = call(
         gram_kernel,
         (jax.ShapeDtypeStruct((rows, vecs), f32), part, part),
-        9,
-        flops=6 * rows * wide * vecs + 4 * rows * vecs * vecs,
+        10,
+        flops=6 * rows * rows * vecs + 4 * rows * vecs * vecs,
         moved=rows * wide * 4 + 20 * rows * vecs,
         name="gram",
-    )(high, low, first, first_core, first_chip, start_basis, coef, other, odd)
+    )(high, low, first, near(first), first_core, first_chip, start_basis, coef, other, odd)
 
     total = mine + lax.ppermute(theirs, "row", core_pairs)
     steps = [1 << bit for bit in range(1, (devices - 1).bit_length())]
@@ -248,6 +270,8 @@
         functools.partial(finish_kernel, row_scale),
         jax.ShapeDtypeStruct((rows, vecs), f32),
         4,
+        out_any=True,
+        scratch=[pltpu.VMEM((rows, vecs), f32), pltpu.SemaphoreType.DMA((2,))],
         flops=18 * vecs**3,
         moved=8 * rows * vecs + 4 * vecs * vecs,
         name="finish",

time: 37 us -> 36.7 us (level)
    pallas_call x1 -> x2, Pallas kernels: 0.5 us -> 0.77 us  [the longest x1 0.5 us: on_device(): call(sweep_kernel, square, 5, flops=6 * rows * rows * vecs, moved=4 * row...]
  transfers between devices with their start and end apart: 11 -> 11, of which waited for: 9 -> 9; matrix products, arithmetic and copies ran while one was open for 2% -> 2% of each run, Pallas kernels for 2% -> 3%
where the time goes in v4:
time: 36.7 us; the launch traced here: 36.5 us
  starting transfers between devices  18.2 us (50%)
  waiting for transfers between devices  10.9 us (30%)
  Pallas kernels  4.14 us (11%)
  local copies, waits for them, and re-layouts  2.52 us (7%)
  other arithmetic  0.77 us (2%)
    ppermute x2, starting transfers between devices, halo(): chip = lax.ppermute(block, 'row', chip_pairs)  9.94 us
    ppermute x4, starting transfers between devices, on_device(): lax.ppermute(total, 'row', [(i, i ^ step) for i in range(devices)])  6.2 us
    ppermute x4, waiting for transfers between devices, on_device(): lax.ppermute(total, 'row', [(i, i ^ step) for i in range(devices)])  6.09 us
    unnamed x12, local copies, waits for them, and re-layouts  2.52 us
    ppermute x1, waiting for transfers between devices, on_device(): moved = lax.ppermute(coef, 'node', [(i, i ^ shift) for i in range(nodes)])  1.84 us
    pallas_call x1, Pallas kernels, on_device(): call(functools.partial(finish_kernel, row_scale), jax.ShapeDtypeStruct((r...  1.75 us
    ppermute x1, starting transfers between devices, on_device(): moved = lax.ppermute(coef, 'node', [(i, i ^ shift) for i in range(nodes)])  1.49 us
    ppermute x1, waiting for transfers between devices, on_device(): theirs = lax.ppermute(total, 'row', core_pairs)  1.25 us
  transfers between devices with their start and end apart: 11, of which 9 were waited for; matrix products, arithmetic and copies ran while one was open for 2% of the time, Pallas kernels for 3%

profile of v4, /device:TPU:0, one launch (start us, length us, event | category | flops | bytes accessed | tf_op | source)
XLA Modules:
  0.0 36.5 jit_solution(15556312982354785426)
XLA Ops:
  0.0 5.4 %collective-permute-start.1 = (f32[256,256]{1,0:T(8,128)}, f32[256,256]{1,0:T(8,128)S(1)}, u32[]{:S(2)}, u32[]{:S(2)}) collective-permute-start(f32[256,256]{1,0:T(8,128)} %start_ref.1), channel_id=1, source_target_pairs={{0,15},{1,2},{2,1},{3,4},{4,3},{5,6},{6,5},{7,8},{8,7},{9,10},{10,... | collective-permute-start | bytes 786440 | tf_op jit(solution)/shard_map/ppermute | solution.py:195
  5.4 0.0 collective-permute-start
  5.4 0.7 %fusion.2 = (f32[1,3]{1,0:T(1,128)S(1)}, f32[3]{0:T(128)S(1)}, f32[3]{0:T(128)S(1)}) fusion(s32[3]{0:T(128)} %param.15, f32[3]{0:T(128)} %param.14, f32[3]{0:T(128)} %param.13, f32[3]{0:T(128)} %param.11, f32[3]{0:T(128)} %param.12), kind=kLoop, calls=%fused_computation.6 | loop fusion | flops 66 | bytes 96 | tf_op jit(solution)/shard_map/broadcast_in_dim | solution.py:206
  6.2 0.0 copy-start.3
  6.2 0.0 copy-start.4
  6.2 0.0 copy-start.5
  6.2 0.6 %copy-done.3 = s32[3]{0:T(128)S(1)} copy-done((s32[3]{0:T(128)S(1)}, s32[3]{0:T(128)}, u32[]{:S(2)}) %copy-start.3) | copy-done | bytes 36
  6.8 0.0 copy-done.4
  6.9 0.0 copy-done.5
  6.9 0.0 copy-start.2
  6.9 0.7 %copy-done.2 = s32[2,7]{1,0:T(2,128)S(1)} copy-done((s32[2,7]{1,0:T(2,128)S(1)}, s32[2,7]{1,0:T(2,128)}, u32[]{:S(2)}) %copy-start.2) | copy-done | bytes 80
  7.6 0.0 copy-start.1
  7.6 1.2 %copy-done.1 = f32[2,7,128,128]{3,2,1,0:T(8,128)S(1)} copy-done((f32[2,7,128,128]{3,2,1,0:T(8,128)S(1)}, f32[2,7,128,128]{3,2,1,0:T(8,128)}, u32[]{:S(2)}) %copy-start.1) | copy-done | bytes 917528
  8.7 0.0 copy-start
  8.7 0.9 %prepare.1 = (bf16[256,768]{1,0:T(8,128)(2,1)S(1)}, bf16[256,768]{1,0:T(8,128)(2,1)S(1)}, s32[8,128]{1,0:T(8,128)S(1)}, f32[8,128]{1,0:T(8,128)S(1)}) custom-call(s32[2,7]{1,0:T(2,128)S(1)} %copy-done.2, f32[1,3]{1,0:T(1,128)S(1)} %get-tuple-element.27.refs_0_, f32[1,3]{1,0:T(1,128)S(1)} %get-tuple-element.26.refs_1_, f32[1,3]{1,0:T(1,128)S(1)} %get-tuple-element.23.refs_2_, ...), custom_call_target="tpu_custom_call" | custom-call | flops 917504 | bytes 2490368 | tf_op jit(solution)/shard_map/prepare/pallas_call | solution.py:213
  9.6 0.2 collective-permute-done.1.chip_ref
  9.8 0.0 collective-permute-done.core_ref
  9.8 0.0 copy-done
  9.8 0.5 %sweep.1.own_ref = f32[256,256]{1,0:T(8,128)S(1)} custom-call(bf16[256,768]{1,0:T(8,128)(2,1)S(1)} %get-tuple-element.14.high_ref, bf16[256,768]{1,0:T(8,128)(2,1)S(1)} %get-tuple-element.15.low_ref, f32[256,256]{1,0:T(8,128)S(1)} %copy-done, f32[256,256]{1,0:T(8,128)S(1)} %collective-permute-done.core_ref, f32[256,256]{1,0:T(8,128)S(1)} %collective-permute-done.1.chip_ref), custom_call_target="tpu_custom_call" | custom-call | flops 100663296 | bytes 1048576 | tf_op jit(solution)/shard_map/sweep/pallas_call | solution.py:237
  10.3 4.5 %collective-permute-start.3 = (f32[256,256]{1,0:T(8,128)S(1)}, f32[256,256]{1,0:T(8,128)S(1)}, u32[]{:S(2)}, u32[]{:S(2)}) collective-permute-start(f32[256,256]{1,0:T(8,128)S(1)} %sweep.1.own_ref), channel_id=1, source_target_pairs={{0,15},{1,2},{2,1},{3,4},{4,3},{5,6},{6,5},{7,8},{8,7},{9,10},{10,... | collective-permute-start | bytes 786440 | tf_op jit(solution)/shard_map/ppermute | solution.py:195
  14.8 0.0 collective-permute-start.2
  14.8 1.5 %collective-permute-start.4 = (f32[8,128]{1,0:T(8,128)S(1)}, f32[8,128]{1,0:T(8,128)S(1)}, u32[]{:S(2)}, u32[]{:S(2)}) collective-permute-start(f32[8,128]{1,0:T(8,128)S(1)} %get-tuple-element.18.coef_ref), channel_id=1, source_target_pairs={{0,16},{16,0},{1,17},{17,1},{2,18},{18,2},{3,19},{19,3},{4,20},{20... | collective-permute-start | bytes 12296 | tf_op jit(solution)/shard_map/ppermute | solution.py:245
  16.3 0.3 near.1.near_ref
  16.6 1.8 %collective-permute-done.4.other_ref = f32[8,128]{1,0:T(8,128)S(1)} collective-permute-done((f32[8,128]{1,0:T(8,128)S(1)}, f32[8,128]{1,0:T(8,128)S(1)}, u32[]{:S(2)}, u32[]{:S(2)}) %collective-permute-start.4) | collective-permute-done | bytes 4128 | tf_op jit(solution)/shard_map/ppermute | solution.py:245
  18.4 0.6 %collective-permute-done.3.chip_ref = f32[256,256]{1,0:T(8,128)S(1)} collective-permute-done((f32[256,256]{1,0:T(8,128)S(1)}, f32[256,256]{1,0:T(8,128)S(1)}, u32[]{:S(2)}, u32[]{:S(2)}) %collective-permute-start.3) | collective-permute-done | bytes 262176 | tf_op jit(solution)/shard_map/ppermute | solution.py:195
  19.0 0.0 collective-permute-done.2.core_ref
  19.0 0.8 %gram.1 = (f32[256,256]{1,0:T(8,128)S(1)}, f32[136,128]{1,0:T(8,128)S(1)}, f32[136,128]{1,0:T(8,128)S(1)}) custom-call(bf16[256,768]{1,0:T(8,128)(2,1)S(1)} %get-tuple-element.14.high_ref, bf16[256,768]{1,0:T(8,128)(2,1)S(1)} %get-tuple-element.15.low_ref, f32[256,256]{1,0:T(8,128)S(1)} %sweep.1.own_ref, f32[256,256]{1,0:T(8,128)S(1)} %near.1.near_ref, ...), custom_call_target="tpu_custom_call" | custom-call | flops 167772160 | bytes 2097152 | tf_op jit(solution)/shard_map/gram/pallas_call | solution.py:250
  19.8 0.5 %collective-permute-start.5 = (f32[136,128]{1,0:T(8,128)S(1)}, f32[136,128]{1,0:T(8,128)S(1)}, u32[]{:S(2)}, u32[]{:S(2)}) collective-permute-start(f32[136,128]{1,0:T(8,128)S(1)} %get-tuple-element.22), channel_id=1, source_target_pairs={{0,1},{1,0},{2,3},{3,2},{4,5},{5,4},{6,7},{7,6},{8,9},{9,8},{10,11... | collective-permute-start | bytes 208904 | tf_op jit(solution)/shard_map/ppermute | solution.py:259
  20.2 0.9 %collective-permute-done.5 = f32[136,128]{1,0:T(8,128)S(1)} collective-permute-done((f32[136,128]{1,0:T(8,128)S(1)}, f32[136,128]{1,0:T(8,128)S(1)}, u32[]{:S(2)}, u32[]{:S(2)}) %collective-permute-start.5) | collective-permute-done | bytes 69664 | tf_op jit(solution)/shard_map/ppermute | solution.py:259
  21.1 2.1 %collective-permute-start.8 = (f32[136,128]{1,0:T(8,128)S(1)}, f32[136,128]{1,0:T(8,128)S(1)}, u32[]{:S(2)}, u32[]{:S(2)}) collective-permute-start(f32[136,128]{1,0:T(8,128)S(1)} %add.27), channel_id=1, source_target_pairs={{0,6},{1,7},{2,4},{3,5},{4,2},{5,3},{6,0},{7,1},{8,14},{9,15},{10,... | collective-permute-start | bytes 208904 | tf_op jit(solution)/shard_map/ppermute | solution.py:264
  23.3 0.4 %collective-permute-start.7 = (f32[136,128]{1,0:T(8,128)S(1)}, f32[136,128]{1,0:T(8,128)S(1)}, u32[]{:S(2)}, u32[]{:S(2)}) collective-permute-start(f32[136,128]{1,0:T(8,128)S(1)} %add.27), channel_id=1, source_target_pairs={{0,4},{1,5},{2,6},{3,7},{4,0},{5,1},{6,2},{7,3},{8,12},{9,13},{10,... | collective-permute-start | bytes 208904 | tf_op jit(solution)/shard_map/ppermute | solution.py:264
  23.7 1.0 %collective-permute-start.6 = (f32[136,128]{1,0:T(8,128)S(1)}, f32[136,128]{1,0:T(8,128)S(1)}, u32[]{:S(2)}, u32[]{:S(2)}) collective-permute-start(f32[136,128]{1,0:T(8,128)S(1)} %add.27), channel_id=1, source_target_pairs={{0,2},{1,3},{2,0},{3,1},{4,6},{5,7},{6,4},{7,5},{8,10},{9,11},{10,... | collective-permute-start | bytes 208904 | tf_op jit(solution)/shard_map/ppermute | solution.py:264
  24.7 2.4 %collective-permute-done.8 = f32[136,128]{1,0:T(8,128)S(1)} collective-permute-done((f32[136,128]{1,0:T(8,128)S(1)}, f32[136,128]{1,0:T(8,128)S(1)}, u32[]{:S(2)}, u32[]{:S(2)}) %collective-permute-start.8) | collective-permute-done | bytes 69664 | tf_op jit(solution)/shard_map/ppermute | solution.py:264
  27.1 0.5 %collective-permute-done.7 = f32[136,128]{1,0:T(8,128)S(1)} collective-permute-done((f32[136,128]{1,0:T(8,128)S(1)}, f32[136,128]{1,0:T(8,128)S(1)}, u32[]{:S(2)}, u32[]{:S(2)}) %collective-permute-start.7) | collective-permute-done | bytes 69664 | tf_op jit(solution)/shard_map/ppermute | solution.py:264
  27.6 0.5 %collective-permute-done.6 = f32[136,128]{1,0:T(8,128)S(1)} collective-permute-done((f32[136,128]{1,0:T(8,128)S(1)}, f32[136,128]{1,0:T(8,128)S(1)}, u32[]{:S(2)}, u32[]{:S(2)}) %collective-permute-start.6) | collective-permute-done | bytes 69664 | tf_op jit(solution)/shard_map/ppermute | solution.py:264
  28.1 2.7 %collective-permute-start.9 = (f32[136,128]{1,0:T(8,128)S(1)}, f32[136,128]{1,0:T(8,128)S(1)}, u32[]{:S(2)}, u32[]{:S(2)}) collective-permute-start(f32[136,128]{1,0:T(8,128)S(1)} %add_add_fusion), channel_id=1, source_target_pairs={{0,8},{1,9},{2,10},{3,11},{4,12},{5,13},{6,14},{7,15},{8,0},{9,1},... | collective-permute-start | bytes 208904 | tf_op jit(solution)/shard_map/ppermute | solution.py:264
  30.7 2.8 %collective-permute-done.9 = f32[136,128]{1,0:T(8,128)S(1)} collective-permute-done((f32[136,128]{1,0:T(8,128)S(1)}, f32[136,128]{1,0:T(8,128)S(1)}, u32[]{:S(2)}, u32[]{:S(2)}) %collective-permute-start.9) | collective-permute-done | bytes 69664 | tf_op jit(solution)/shard_map/ppermute | solution.py:264
  33.5 0.1 collective-permute-start.10
  33.5 1.2 %collective-permute-done.10.theirs_ref = f32[136,128]{1,0:T(8,128)S(1)} collective-permute-done((f32[136,128]{1,0:T(8,128)S(1)}, f32[136,128]{1,0:T(8,128)S(1)}, u32[]{:S(2)}, u32[]{:S(2)}) %collective-permute-start.10) | collective-permute-done | bytes 69664 | tf_op jit(solution)/shard_map/ppermute | solution.py:267
  34.8 1.8 %finish.1 = f32[256,256]{1,0:T(8,128)} custom-call(f32[256,256]{1,0:T(8,128)S(1)} %get-tuple-element.20.filtered_ref, f32[136,128]{1,0:T(8,128)S(1)} %add.31.mine_ref, f32[136,128]{1,0:T(8,128)S(1)} %collective-permute-done.10.theirs_ref, s32[8,128]{1,0:T(8,128)S(1)} %get-tuple-element.19.odd_ref), custom_call_target="tpu_custom_call" | custom-call | flops 301989888 | bytes 786432 | tf_op jit(solution)/shard_map/finish/pallas_call | solution.py:269
  (4 shorter events, 0.0 us)
Async XLA Ops:
  0.0 9.8 %collective-permute-start.1 = (f32[256,256]{1,0:T(8,128)}, f32[256,256]{1,0:T(8,128)S(1)}, u32[]{:S(2)}, u32[]{:S(2)}) collective-permute-start(f32[256,256]{1,0:T(8,128)} %start_ref.1), channel_id=1, source_target_pairs={{0,15},{1,2},{2,1},{3,4},{4,3},{5,6},{6,5},{7,8},{8,7},{9,10},{10,... | collective-permute-start | bytes 786440 | tf_op jit(solution)/shard_map/ppermute | solution.py:195
  5.4 4.4 %collective-permute-start = (f32[256,256]{1,0:T(8,128)}, f32[256,256]{1,0:T(8,128)S(1)}, u32[]{:S(2)}, u32[]{:S(2)}) collective-permute-start(f32[256,256]{1,0:T(8,128)} %start_ref.1), channel_id=1, source_target_pairs={{0,1},{1,0},{2,3},{3,2},{4,5},{5,4},{6,7},{7,6},{8,9},{9,8},{10,11... | collective-permute-start | bytes 786440 | tf_op jit(solution)/shard_map/ppermute | solution.py:196
  6.2 0.7 %copy-start.3 = (s32[3]{0:T(128)S(1)}, s32[3]{0:T(128)}, u32[]{:S(2)}) copy-start(s32[3]{0:T(128)} %param.15) | copy-start | bytes 40
  6.2 0.7 %copy-start.4 = (f32[3]{0:T(128)S(1)}, f32[3]{0:T(128)}, u32[]{:S(2)}) copy-start(f32[3]{0:T(128)} %param.14) | copy-start | bytes 40
  6.2 0.7 %copy-start.5 = (f32[3]{0:T(128)S(1)}, f32[3]{0:T(128)}, u32[]{:S(2)}) copy-start(f32[3]{0:T(128)} %param.13) | copy-start | bytes 40
  6.9 0.7 %copy-start.2 = (s32[2,7]{1,0:T(2,128)S(1)}, s32[2,7]{1,0:T(2,128)}, u32[]{:S(2)}) copy-start(s32[2,7]{1,0:T(2,128)} %cols_ref.1) | copy-start | bytes 172
  7.6 1.2 %copy-start.1 = (f32[2,7,128,128]{3,2,1,0:T(8,128)S(1)}, f32[2,7,128,128]{3,2,1,0:T(8,128)}, u32[]{:S(2)}) copy-start(f32[2,7,128,128]{3,2,1,0:T(8,128)} %refs_3_.1) | copy-start | bytes 2752516
  8.7 1.1 %copy-start = (f32[256,256]{1,0:T(8,128)S(1)}, f32[256,256]{1,0:T(8,128)}, u32[]{:S(2)}) copy-start(f32[256,256]{1,0:T(8,128)} %start_ref.1) | copy-start | bytes 786436
  10.3 8.7 %collective-permute-start.3 = (f32[256,256]{1,0:T(8,128)S(1)}, f32[256,256]{1,0:T(8,128)S(1)}, u32[]{:S(2)}, u32[]{:S(2)}) collective-permute-start(f32[256,256]{1,0:T(8,128)S(1)} %sweep.1.own_ref), channel_id=1, source_target_pairs={{0,15},{1,2},{2,1},{3,4},{4,3},{5,6},{6,5},{7,8},{8,7},{9,10},{10,... | collective-permute-start | bytes 786440 | tf_op jit(solution)/shard_map/ppermute | solution.py:195
  14.8 4.2 %collective-permute-start.2 = (f32[256,256]{1,0:T(8,128)S(1)}, f32[256,256]{1,0:T(8,128)S(1)}, u32[]{:S(2)}, u32[]{:S(2)}) collective-permute-start(f32[256,256]{1,0:T(8,128)S(1)} %sweep.1.own_ref), channel_id=1, source_target_pairs={{0,1},{1,0},{2,3},{3,2},{4,5},{5,4},{6,7},{7,6},{8,9},{9,8},{10,11... | collective-permute-start | bytes 786440 | tf_op jit(solution)/shard_map/ppermute | solution.py:196
  14.8 3.6 %collective-permute-start.4 = (f32[8,128]{1,0:T(8,128)S(1)}, f32[8,128]{1,0:T(8,128)S(1)}, u32[]{:S(2)}, u32[]{:S(2)}) collective-permute-start(f32[8,128]{1,0:T(8,128)S(1)} %get-tuple-element.18.coef_ref), channel_id=1, source_target_pairs={{0,16},{16,0},{1,17},{17,1},{2,18},{18,2},{3,19},{19,3},{4,20},{20... | collective-permute-start | bytes 12296 | tf_op jit(solution)/shard_map/ppermute | solution.py:245
  19.8 1.4 %collective-permute-start.5 = (f32[136,128]{1,0:T(8,128)S(1)}, f32[136,128]{1,0:T(8,128)S(1)}, u32[]{:S(2)}, u32[]{:S(2)}) collective-permute-start(f32[136,128]{1,0:T(8,128)S(1)} %get-tuple-element.22), channel_id=1, source_target_pairs={{0,1},{1,0},{2,3},{3,2},{4,5},{5,4},{6,7},{7,6},{8,9},{9,8},{10,11... | collective-permute-start | bytes 208904 | tf_op jit(solution)/shard_map/ppermute | solution.py:259
  21.1 6.0 %collective-permute-start.8 = (f32[136,128]{1,0:T(8,128)S(1)}, f32[136,128]{1,0:T(8,128)S(1)}, u32[]{:S(2)}, u32[]{:S(2)}) collective-permute-start(f32[136,128]{1,0:T(8,128)S(1)} %add.27), channel_id=1, source_target_pairs={{0,6},{1,7},{2,4},{3,5},{4,2},{5,3},{6,0},{7,1},{8,14},{9,15},{10,... | collective-permute-start | bytes 208904 | tf_op jit(solution)/shard_map/ppermute | solution.py:264
  23.3 4.3 %collective-permute-start.7 = (f32[136,128]{1,0:T(8,128)S(1)}, f32[136,128]{1,0:T(8,128)S(1)}, u32[]{:S(2)}, u32[]{:S(2)}) collective-permute-start(f32[136,128]{1,0:T(8,128)S(1)} %add.27), channel_id=1, source_target_pairs={{0,4},{1,5},{2,6},{3,7},{4,0},{5,1},{6,2},{7,3},{8,12},{9,13},{10,... | collective-permute-start | bytes 208904 | tf_op jit(solution)/shard_map/ppermute | solution.py:264
  23.7 4.3 %collective-permute-start.6 = (f32[136,128]{1,0:T(8,128)S(1)}, f32[136,128]{1,0:T(8,128)S(1)}, u32[]{:S(2)}, u32[]{:S(2)}) collective-permute-start(f32[136,128]{1,0:T(8,128)S(1)} %add.27), channel_id=1, source_target_pairs={{0,2},{1,3},{2,0},{3,1},{4,6},{5,7},{6,4},{7,5},{8,10},{9,11},{10,... | collective-permute-start | bytes 208904 | tf_op jit(solution)/shard_map/ppermute | solution.py:264
  28.1 5.4 %collective-permute-start.9 = (f32[136,128]{1,0:T(8,128)S(1)}, f32[136,128]{1,0:T(8,128)S(1)}, u32[]{:S(2)}, u32[]{:S(2)}) collective-permute-start(f32[136,128]{1,0:T(8,128)S(1)} %add_add_fusion), channel_id=1, source_target_pairs={{0,8},{1,9},{2,10},{3,11},{4,12},{5,13},{6,14},{7,15},{8,0},{9,1},... | collective-permute-start | bytes 208904 | tf_op jit(solution)/shard_map/ppermute | solution.py:264
  33.5 1.3 %collective-permute-start.10 = (f32[136,128]{1,0:T(8,128)S(1)}, f32[136,128]{1,0:T(8,128)S(1)}, u32[]{:S(2)}, u32[]{:S(2)}) collective-permute-start(f32[136,128]{1,0:T(8,128)S(1)} %add.31.mine_ref), channel_id=1, source_target_pairs={{0,1},{1,0},{2,3},{3,2},{4,5},{5,4},{6,7},{7,6},{8,9},{9,8},{10,11... | collective-permute-start | bytes 208904 | tf_op jit(solution)/shard_map/ppermute | solution.py:267

commit v5 on v4

--- a/solution.py
+++ b/solution.py
@@ -82,9 +82,26 @@
     out_ref[...] = banded(high_ref, low_ref, 0, (own_ref, core_ref, chip_ref))
 
 
-def gram_kernel(
+def gram_piece(filtered, take_second, out_ref):
+    half = out_ref.shape[1]
+    one, two = filtered[:, :half], filtered[:, half:]
+    x_high, x_low = split(jnp.where(take_second, two, one))
+    y_high, y_low = split(jnp.where(take_second, one, two))
+    high = jnp.concatenate([x_high, y_high], axis=1)
+    low = jnp.concatenate([x_low, y_low], axis=1)
+    rows = ((0,), (0,))
+    both = mm(x_high, high, rows) + (mm(x_high, low, rows) + mm(x_low, high, rows))
+    same, cross = both[:, :half], both[:, half:]
+    row = lax.broadcasted_iota(jnp.int32, (half, half), 0)
+    col = lax.broadcasted_iota(jnp.int32, (half, half), 1)
+    out_ref[:half] = jnp.where(col >= row, same, cross)
+    diagonal = jnp.sum(jnp.where(col == row, cross, 0.0), axis=0, keepdims=True)
+    out_ref[half:] = jnp.broadcast_to(diagonal, (SUBLANES, half))
+
+
+def filter_kernel(
     high_ref, low_ref, own_ref, near_ref, core_ref, chip_ref, start_ref, coef_ref, other_ref, odd_ref,
-    filtered_ref, mine_ref, theirs_ref,
+    filtered_ref, theirs_ref,
 ):
     second = near_ref[...] + banded(high_ref, low_ref, 1, (core_ref, chip_ref))
     coef = coef_ref[...] + other_ref[...]
@@ -92,40 +109,31 @@
         coef[0:1, 0:1] * start_ref[...] + coef[1:2, 0:1] * own_ref[...] + coef[2:3, 0:1] * second
     )
     filtered_ref[...] = filtered
-    high, low = split(filtered)
-    cross = mm(high, low, ((0,), (0,)))
-    gram = mm(high, high, ((0,), (0,))) + (cross + cross.T)
-    half = gram.shape[0] // 2
-    row = lax.broadcasted_iota(jnp.int32, (half, half), 0)
-    col = lax.broadcasted_iota(jnp.int32, (half, half), 1)
-    upper, lower, side = gram[:half, :half], gram[half:, half:], gram[:half, half:]
-    packed = jnp.where(col >= row, upper, lower)
-    diagonal = jnp.sum(jnp.where(col == row, lower, 0.0), axis=0, keepdims=True)
-    diagonal = jnp.broadcast_to(diagonal, (SUBLANES, half))
-    odd = odd_ref[0:1, 0:1] == 1
-    mine_ref[:half] = jnp.where(odd, packed, side)
-    theirs_ref[:half] = jnp.where(odd, side, packed)
-    mine_ref[half:] = diagonal
-    theirs_ref[half:] = diagonal
+    gram_piece(filtered, odd_ref[0:1, 0:1] == 0, theirs_ref)
+
+
+def mine_kernel(filtered_ref, odd_ref, mine_ref):
+    gram_piece(filtered_ref[...], odd_ref[0:1, 0:1] == 1, mine_ref)
 
 
 def finish_kernel(row_scale, filtered_ref, mine_ref, theirs_ref, odd_ref, out_ref, held, sems):
     half = mine_ref.shape[1]
     odd = odd_ref[0:1, 0:1] == 1
     mine, theirs = mine_ref[...], theirs_ref[...]
-    packed = jnp.where(odd, mine, theirs)
-    side = jnp.where(odd, theirs, mine)[:half]
-    diagonal = packed[half:half + 1]
-    packed = packed[:half]
+    one, two = jnp.where(odd, theirs, mine), jnp.where(odd, mine, theirs)
+    diagonal = one[half:half + 1]
+    one, two = one[:half], two[:half]
     row = lax.broadcasted_iota(jnp.int32, (half, half), 0)
     col = lax.broadcasted_iota(jnp.int32, (half, half), 1)
-    turned = packed.T
-    upper = jnp.where(col >= row, packed, turned)
-    lower = jnp.where(col < row, packed, jnp.where(col > row, turned, diagonal))
+    one_turned, two_turned = one.T, two.T
+    upper = jnp.where(col >= row, one, one_turned)
+    lower = jnp.where(col >= row, two, two_turned)
+    side = jnp.where(col < row, one, jnp.where(col > row, two_turned, diagonal))
+    side_turned = jnp.where(col < row, two, jnp.where(col > row, one_turned, diagonal))
     gram = jnp.concatenate(
         [
             jnp.concatenate([upper, side], axis=1),
-            jnp.concatenate([side.T, lower], axis=1),
+            jnp.concatenate([side_turned, lower], axis=1),
         ],
         axis=0,
     )
@@ -247,16 +255,16 @@
 
     half = vecs // 2
     part = jax.ShapeDtypeStruct((half + SUBLANES, half), f32)
-    filtered, mine, theirs = call(
-        gram_kernel,
-        (jax.ShapeDtypeStruct((rows, vecs), f32), part, part),
-        10,
-        flops=6 * rows * rows * vecs + 4 * rows * vecs * vecs,
-        moved=rows * wide * 4 + 20 * rows * vecs,
-        name="gram",
+    filtered, theirs = call(
+        filter_kernel, (square, part), 10,
+        flops=12 * rows * rows * vecs + 2 * rows * vecs * vecs,
+        moved=rows * wide * 4 + 24 * rows * vecs, name="filter",
     )(high, low, first, near(first), first_core, first_chip, start_basis, coef, other, odd)
-
-    total = mine + lax.ppermute(theirs, "row", core_pairs)
+    swapped = lax.ppermute(theirs, "row", core_pairs)
+    mine = call(
+        mine_kernel, part, 2, flops=2 * rows * vecs * vecs, moved=6 * rows * vecs, name="mine"
+    )(filtered, odd)
+    total = mine + swapped
     steps = [1 << bit for bit in range(1, (devices - 1).bit_length())]
     phases = [[steps[0], steps[1], steps[0] + steps[1]]] if len(steps) > 1 else [steps]
     for phase in phases + [[step] for step in steps[2:]]:

time: 36.7 us -> 36.7 us (level)
    pallas_call x1 -> x2, Pallas kernels: 0.76 us -> 1.02 us  [the longest x1 0.73 us: on_device(): call(filter_kernel, (square, part), 10, flops=12 * rows * rows * vecs + 2...]
  transfers between devices with their start and end apart: 11 -> 11, of which waited for: 9 -> 9; matrix products, arithmetic and copies ran while one was open for 2% -> 2% of each run, Pallas kernels for 3% -> 4%
where the time goes in v5:
time: 36.7 us; the launch traced here: 36.5 us
  starting transfers between devices  18.2 us (50%)
  waiting for transfers between devices  10.6 us (29%)
  Pallas kernels  4.39 us (12%)
  local copies, waits for them, and re-layouts  2.52 us (7%)
  other arithmetic  0.78 us (2%)
    ppermute x2, starting transfers between devices, halo(): chip = lax.ppermute(block, 'row', chip_pairs)  9.95 us
    ppermute x4, starting transfers between devices, on_device(): lax.ppermute(total, 'row', [(i, i ^ step) for i in range(devices)])  6.21 us
    ppermute x4, waiting for transfers between devices, on_device(): lax.ppermute(total, 'row', [(i, i ^ step) for i in range(devices)])  6.09 us
    unnamed x12, local copies, waits for them, and re-layouts  2.52 us
    ppermute x1, waiting for transfers between devices, on_device(): moved = lax.ppermute(coef, 'node', [(i, i ^ shift) for i in range(nodes)])  1.85 us
    pallas_call x1, Pallas kernels, on_device(): call(functools.partial(finish_kernel, row_scale), jax.ShapeDtypeStruct((r...  1.76 us
    ppermute x1, starting transfers between devices, on_device(): moved = lax.ppermute(coef, 'node', [(i, i ^ shift) for i in range(nodes)])  1.49 us
    ppermute x1, waiting for transfers between devices, on_device(): theirs = lax.ppermute(total, 'row', core_pairs)  1.25 us
  transfers between devices with their start and end apart: 11, of which 9 were waited for; matrix products, arithmetic and copies ran while one was open for 2% of the time, Pallas kernels for 4%

profile of v5, /device:TPU:0, one launch (start us, length us, event | category | flops | bytes accessed | tf_op | source)
XLA Modules:
  0.0 36.5 jit_solution(8271039452583754461)
XLA Ops:
  0.0 5.4 %collective-permute-start.1 = (f32[256,256]{1,0:T(8,128)}, f32[256,256]{1,0:T(8,128)S(1)}, u32[]{:S(2)}, u32[]{:S(2)}) collective-permute-start(f32[256,256]{1,0:T(8,128)} %start_ref.1), channel_id=1, source_target_pairs={{0,15},{1,2},{2,1},{3,4},{4,3},{5,6},{6,5},{7,8},{8,7},{9,10},{10,... | collective-permute-start | bytes 786440 | tf_op jit(solution)/shard_map/ppermute | solution.py:203
  5.4 0.0 collective-permute-start
  5.4 0.7 %fusion.2 = (f32[1,3]{1,0:T(1,128)S(1)}, f32[3]{0:T(128)S(1)}, f32[3]{0:T(128)S(1)}) fusion(s32[3]{0:T(128)} %param.15, f32[3]{0:T(128)} %param.14, f32[3]{0:T(128)} %param.13, f32[3]{0:T(128)} %param.11, f32[3]{0:T(128)} %param.12), kind=kLoop, calls=%fused_computation.6 | loop fusion | flops 66 | bytes 96 | tf_op jit(solution)/shard_map/broadcast_in_dim | solution.py:214
  6.2 0.0 copy-start.3
  6.2 0.0 copy-start.4
  6.2 0.0 copy-start.5
  6.2 0.6 %copy-done.3 = s32[3]{0:T(128)S(1)} copy-done((s32[3]{0:T(128)S(1)}, s32[3]{0:T(128)}, u32[]{:S(2)}) %copy-start.3) | copy-done | bytes 36
  6.8 0.0 copy-done.4
  6.9 0.0 copy-done.5
  6.9 0.0 copy-start.2
  6.9 0.7 %copy-done.2 = s32[2,7]{1,0:T(2,128)S(1)} copy-done((s32[2,7]{1,0:T(2,128)S(1)}, s32[2,7]{1,0:T(2,128)}, u32[]{:S(2)}) %copy-start.2) | copy-done | bytes 80
  7.6 0.0 copy-start.1
  7.6 1.2 %copy-done.1 = f32[2,7,128,128]{3,2,1,0:T(8,128)S(1)} copy-done((f32[2,7,128,128]{3,2,1,0:T(8,128)S(1)}, f32[2,7,128,128]{3,2,1,0:T(8,128)}, u32[]{:S(2)}) %copy-start.1) | copy-done | bytes 917528
  8.7 0.0 copy-start
  8.7 0.9 %prepare.1 = (bf16[256,768]{1,0:T(8,128)(2,1)S(1)}, bf16[256,768]{1,0:T(8,128)(2,1)S(1)}, s32[8,128]{1,0:T(8,128)S(1)}, f32[8,128]{1,0:T(8,128)S(1)}) custom-call(s32[2,7]{1,0:T(2,128)S(1)} %copy-done.2, f32[1,3]{1,0:T(1,128)S(1)} %get-tuple-element.25.refs_0_, f32[1,3]{1,0:T(1,128)S(1)} %get-tuple-element.24.refs_1_, f32[1,3]{1,0:T(1,128)S(1)} %get-tuple-element.21.refs_2_, ...), custom_call_target="tpu_custom_call" | custom-call | flops 917504 | bytes 2490368 | tf_op jit(solution)/shard_map/prepare/pallas_call | solution.py:221
  9.6 0.2 collective-permute-done.1.chip_ref
  9.8 0.0 collective-permute-done.core_ref
  9.8 0.0 copy-done
  9.8 0.5 %sweep.1.own_ref = f32[256,256]{1,0:T(8,128)S(1)} custom-call(bf16[256,768]{1,0:T(8,128)(2,1)S(1)} %get-tuple-element.13.high_ref, bf16[256,768]{1,0:T(8,128)(2,1)S(1)} %get-tuple-element.14.low_ref, f32[256,256]{1,0:T(8,128)S(1)} %copy-done, f32[256,256]{1,0:T(8,128)S(1)} %collective-permute-done.core_ref, f32[256,256]{1,0:T(8,128)S(1)} %collective-permute-done.1.chip_ref), custom_call_target="tpu_custom_call" | custom-call | flops 100663296 | bytes 1048576 | tf_op jit(solution)/shard_map/sweep/pallas_call | solution.py:245
  10.3 4.5 %collective-permute-start.3 = (f32[256,256]{1,0:T(8,128)S(1)}, f32[256,256]{1,0:T(8,128)S(1)}, u32[]{:S(2)}, u32[]{:S(2)}) collective-permute-start(f32[256,256]{1,0:T(8,128)S(1)} %sweep.1.own_ref), channel_id=1, source_target_pairs={{0,15},{1,2},{2,1},{3,4},{4,3},{5,6},{6,5},{7,8},{8,7},{9,10},{10,... | collective-permute-start | bytes 786440 | tf_op jit(solution)/shard_map/ppermute | solution.py:203
  14.8 0.0 collective-permute-start.2
  14.8 1.5 %collective-permute-start.4 = (f32[8,128]{1,0:T(8,128)S(1)}, f32[8,128]{1,0:T(8,128)S(1)}, u32[]{:S(2)}, u32[]{:S(2)}) collective-permute-start(f32[8,128]{1,0:T(8,128)S(1)} %get-tuple-element.17.coef_ref), channel_id=1, source_target_pairs={{0,16},{16,0},{1,17},{17,1},{2,18},{18,2},{3,19},{19,3},{4,20},{20... | collective-permute-start | bytes 12296 | tf_op jit(solution)/shard_map/ppermute | solution.py:253
  16.3 0.3 near.1.near_ref
  16.6 1.8 %collective-permute-done.4.other_ref = f32[8,128]{1,0:T(8,128)S(1)} collective-permute-done((f32[8,128]{1,0:T(8,128)S(1)}, f32[8,128]{1,0:T(8,128)S(1)}, u32[]{:S(2)}, u32[]{:S(2)}) %collective-permute-start.4) | collective-permute-done | bytes 4128 | tf_op jit(solution)/shard_map/ppermute | solution.py:253
  18.4 0.6 %collective-permute-done.3.chip_ref = f32[256,256]{1,0:T(8,128)S(1)} collective-permute-done((f32[256,256]{1,0:T(8,128)S(1)}, f32[256,256]{1,0:T(8,128)S(1)}, u32[]{:S(2)}, u32[]{:S(2)}) %collective-permute-start.3) | collective-permute-done | bytes 262176 | tf_op jit(solution)/shard_map/ppermute | solution.py:203
  19.0 0.0 collective-permute-done.2.core_ref
  19.0 0.7 %filter.1 = (f32[256,256]{1,0:T(8,128)S(1)}, f32[136,128]{1,0:T(8,128)S(1)}) custom-call(bf16[256,768]{1,0:T(8,128)(2,1)S(1)} %get-tuple-element.13.high_ref, bf16[256,768]{1,0:T(8,128)(2,1)S(1)} %get-tuple-element.14.low_ref, f32[256,256]{1,0:T(8,128)S(1)} %sweep.1.own_ref, f32[256,256]{1,0:T(8,128)S(1)} %near.1.near_ref, ...), custom_call_target="tpu_custom_call" | custom-call | flops 234881024 | bytes 2359296 | tf_op jit(solution)/shard_map/filter/pallas_call | solution.py:258
  19.7 0.4 %collective-permute-start.5 = (f32[136,128]{1,0:T(8,128)S(1)}, f32[136,128]{1,0:T(8,128)S(1)}, u32[]{:S(2)}, u32[]{:S(2)}) collective-permute-start(f32[136,128]{1,0:T(8,128)S(1)} %get-tuple-element.20), channel_id=1, source_target_pairs={{0,1},{1,0},{2,3},{3,2},{4,5},{5,4},{6,7},{7,6},{8,9},{9,8},{10,11... | collective-permute-start | bytes 208904 | tf_op jit(solution)/shard_map/ppermute | solution.py:263
  20.2 0.3 mine.1
  20.5 0.6 %collective-permute-done.5 = f32[136,128]{1,0:T(8,128)S(1)} collective-permute-done((f32[136,128]{1,0:T(8,128)S(1)}, f32[136,128]{1,0:T(8,128)S(1)}, u32[]{:S(2)}, u32[]{:S(2)}) %collective-permute-start.5) | collective-permute-done | bytes 69664 | tf_op jit(solution)/shard_map/ppermute | solution.py:263
  21.1 2.1 %collective-permute-start.8 = (f32[136,128]{1,0:T(8,128)S(1)}, f32[136,128]{1,0:T(8,128)S(1)}, u32[]{:S(2)}, u32[]{:S(2)}) collective-permute-start(f32[136,128]{1,0:T(8,128)S(1)} %add.27), channel_id=1, source_target_pairs={{0,6},{1,7},{2,4},{3,5},{4,2},{5,3},{6,0},{7,1},{8,14},{9,15},{10,... | collective-permute-start | bytes 208904 | tf_op jit(solution)/shard_map/ppermute | solution.py:272
  23.2 0.4 %collective-permute-start.7 = (f32[136,128]{1,0:T(8,128)S(1)}, f32[136,128]{1,0:T(8,128)S(1)}, u32[]{:S(2)}, u32[]{:S(2)}) collective-permute-start(f32[136,128]{1,0:T(8,128)S(1)} %add.27), channel_id=1, source_target_pairs={{0,4},{1,5},{2,6},{3,7},{4,0},{5,1},{6,2},{7,3},{8,12},{9,13},{10,... | collective-permute-start | bytes 208904 | tf_op jit(solution)/shard_map/ppermute | solution.py:272
  23.7 1.0 %collective-permute-start.6 = (f32[136,128]{1,0:T(8,128)S(1)}, f32[136,128]{1,0:T(8,128)S(1)}, u32[]{:S(2)}, u32[]{:S(2)}) collective-permute-start(f32[136,128]{1,0:T(8,128)S(1)} %add.27), channel_id=1, source_target_pairs={{0,2},{1,3},{2,0},{3,1},{4,6},{5,7},{6,4},{7,5},{8,10},{9,11},{10,... | collective-permute-start | bytes 208904 | tf_op jit(solution)/shard_map/ppermute | solution.py:272
  24.6 2.4 %collective-permute-done.8 = f32[136,128]{1,0:T(8,128)S(1)} collective-permute-done((f32[136,128]{1,0:T(8,128)S(1)}, f32[136,128]{1,0:T(8,128)S(1)}, u32[]{:S(2)}, u32[]{:S(2)}) %collective-permute-start.8) | collective-permute-done | bytes 69664 | tf_op jit(solution)/shard_map/ppermute | solution.py:272
  27.1 0.5 %collective-permute-done.7 = f32[136,128]{1,0:T(8,128)S(1)} collective-permute-done((f32[136,128]{1,0:T(8,128)S(1)}, f32[136,128]{1,0:T(8,128)S(1)}, u32[]{:S(2)}, u32[]{:S(2)}) %collective-permute-start.7) | collective-permute-done | bytes 69664 | tf_op jit(solution)/shard_map/ppermute | solution.py:272
  27.5 0.4 %collective-permute-done.6 = f32[136,128]{1,0:T(8,128)S(1)} collective-permute-done((f32[136,128]{1,0:T(8,128)S(1)}, f32[136,128]{1,0:T(8,128)S(1)}, u32[]{:S(2)}, u32[]{:S(2)}) %collective-permute-start.6) | collective-permute-done | bytes 69664 | tf_op jit(solution)/shard_map/ppermute | solution.py:272
  28.0 2.7 %collective-permute-start.9 = (f32[136,128]{1,0:T(8,128)S(1)}, f32[136,128]{1,0:T(8,128)S(1)}, u32[]{:S(2)}, u32[]{:S(2)}) collective-permute-start(f32[136,128]{1,0:T(8,128)S(1)} %add_add_fusion), channel_id=1, source_target_pairs={{0,8},{1,9},{2,10},{3,11},{4,12},{5,13},{6,14},{7,15},{8,0},{9,1},... | collective-permute-start | bytes 208904 | tf_op jit(solution)/shard_map/ppermute | solution.py:272
  30.7 2.7 %collective-permute-done.9 = f32[136,128]{1,0:T(8,128)S(1)} collective-permute-done((f32[136,128]{1,0:T(8,128)S(1)}, f32[136,128]{1,0:T(8,128)S(1)}, u32[]{:S(2)}, u32[]{:S(2)}) %collective-permute-start.9) | collective-permute-done | bytes 69664 | tf_op jit(solution)/shard_map/ppermute | solution.py:272
  33.4 0.1 collective-permute-start.10
  33.5 1.2 %collective-permute-done.10.theirs_ref = f32[136,128]{1,0:T(8,128)S(1)} collective-permute-done((f32[136,128]{1,0:T(8,128)S(1)}, f32[136,128]{1,0:T(8,128)S(1)}, u32[]{:S(2)}, u32[]{:S(2)}) %collective-permute-start.10) | collective-permute-done | bytes 69664 | tf_op jit(solution)/shard_map/ppermute | solution.py:275
  34.8 1.8 %finish.1 = f32[256,256]{1,0:T(8,128)} custom-call(f32[256,256]{1,0:T(8,128)S(1)} %get-tuple-element.19.filtered_ref, f32[136,128]{1,0:T(8,128)S(1)} %add.31.mine_ref, f32[136,128]{1,0:T(8,128)S(1)} %collective-permute-done.10.theirs_ref, s32[8,128]{1,0:T(8,128)S(1)} %get-tuple-element.18.odd_ref), custom_call_target="tpu_custom_call" | custom-call | flops 301989888 | bytes 786432 | tf_op jit(solution)/shard_map/finish/pallas_call | solution.py:277
  (4 shorter events, 0.0 us)
Async XLA Ops:
  0.0 9.8 %collective-permute-start.1 = (f32[256,256]{1,0:T(8,128)}, f32[256,256]{1,0:T(8,128)S(1)}, u32[]{:S(2)}, u32[]{:S(2)}) collective-permute-start(f32[256,256]{1,0:T(8,128)} %start_ref.1), channel_id=1, source_target_pairs={{0,15},{1,2},{2,1},{3,4},{4,3},{5,6},{6,5},{7,8},{8,7},{9,10},{10,... | collective-permute-start | bytes 786440 | tf_op jit(solution)/shard_map/ppermute | solution.py:203
  5.4 4.4 %collective-permute-start = (f32[256,256]{1,0:T(8,128)}, f32[256,256]{1,0:T(8,128)S(1)}, u32[]{:S(2)}, u32[]{:S(2)}) collective-permute-start(f32[256,256]{1,0:T(8,128)} %start_ref.1), channel_id=1, source_target_pairs={{0,1},{1,0},{2,3},{3,2},{4,5},{5,4},{6,7},{7,6},{8,9},{9,8},{10,11... | collective-permute-start | bytes 786440 | tf_op jit(solution)/shard_map/ppermute | solution.py:204
  6.2 0.7 %copy-start.3 = (s32[3]{0:T(128)S(1)}, s32[3]{0:T(128)}, u32[]{:S(2)}) copy-start(s32[3]{0:T(128)} %param.15) | copy-start | bytes 40
  6.2 0.7 %copy-start.4 = (f32[3]{0:T(128)S(1)}, f32[3]{0:T(128)}, u32[]{:S(2)}) copy-start(f32[3]{0:T(128)} %param.14) | copy-start | bytes 40
  6.2 0.7 %copy-start.5 = (f32[3]{0:T(128)S(1)}, f32[3]{0:T(128)}, u32[]{:S(2)}) copy-start(f32[3]{0:T(128)} %param.13) | copy-start | bytes 40
  6.9 0.7 %copy-start.2 = (s32[2,7]{1,0:T(2,128)S(1)}, s32[2,7]{1,0:T(2,128)}, u32[]{:S(2)}) copy-start(s32[2,7]{1,0:T(2,128)} %cols_ref.1) | copy-start | bytes 172
  7.6 1.2 %copy-start.1 = (f32[2,7,128,128]{3,2,1,0:T(8,128)S(1)}, f32[2,7,128,128]{3,2,1,0:T(8,128)}, u32[]{:S(2)}) copy-start(f32[2,7,128,128]{3,2,1,0:T(8,128)} %refs_3_.1) | copy-start | bytes 2752516
  8.7 1.1 %copy-start = (f32[256,256]{1,0:T(8,128)S(1)}, f32[256,256]{1,0:T(8,128)}, u32[]{:S(2)}) copy-start(f32[256,256]{1,0:T(8,128)} %start_ref.1) | copy-start | bytes 786436
  10.3 8.7 %collective-permute-start.3 = (f32[256,256]{1,0:T(8,128)S(1)}, f32[256,256]{1,0:T(8,128)S(1)}, u32[]{:S(2)}, u32[]{:S(2)}) collective-permute-start(f32[256,256]{1,0:T(8,128)S(1)} %sweep.1.own_ref), channel_id=1, source_target_pairs={{0,15},{1,2},{2,1},{3,4},{4,3},{5,6},{6,5},{7,8},{8,7},{9,10},{10,... | collective-permute-start | bytes 786440 | tf_op jit(solution)/shard_map/ppermute | solution.py:203
  14.8 4.2 %collective-permute-start.2 = (f32[256,256]{1,0:T(8,128)S(1)}, f32[256,256]{1,0:T(8,128)S(1)}, u32[]{:S(2)}, u32[]{:S(2)}) collective-permute-start(f32[256,256]{1,0:T(8,128)S(1)} %sweep.1.own_ref), channel_id=1, source_target_pairs={{0,1},{1,0},{2,3},{3,2},{4,5},{5,4},{6,7},{7,6},{8,9},{9,8},{10,11... | collective-permute-start | bytes 786440 | tf_op jit(solution)/shard_map/ppermute | solution.py:204
  14.8 3.6 %collective-permute-start.4 = (f32[8,128]{1,0:T(8,128)S(1)}, f32[8,128]{1,0:T(8,128)S(1)}, u32[]{:S(2)}, u32[]{:S(2)}) collective-permute-start(f32[8,128]{1,0:T(8,128)S(1)} %get-tuple-element.17.coef_ref), channel_id=1, source_target_pairs={{0,16},{16,0},{1,17},{17,1},{2,18},{18,2},{3,19},{19,3},{4,20},{20... | collective-permute-start | bytes 12296 | tf_op jit(solution)/shard_map/ppermute | solution.py:253
  19.7 1.4 %collective-permute-start.5 = (f32[136,128]{1,0:T(8,128)S(1)}, f32[136,128]{1,0:T(8,128)S(1)}, u32[]{:S(2)}, u32[]{:S(2)}) collective-permute-start(f32[136,128]{1,0:T(8,128)S(1)} %get-tuple-element.20), channel_id=1, source_target_pairs={{0,1},{1,0},{2,3},{3,2},{4,5},{5,4},{6,7},{7,6},{8,9},{9,8},{10,11... | collective-permute-start | bytes 208904 | tf_op jit(solution)/shard_map/ppermute | solution.py:263
  21.1 6.0 %collective-permute-start.8 = (f32[136,128]{1,0:T(8,128)S(1)}, f32[136,128]{1,0:T(8,128)S(1)}, u32[]{:S(2)}, u32[]{:S(2)}) collective-permute-start(f32[136,128]{1,0:T(8,128)S(1)} %add.27), channel_id=1, source_target_pairs={{0,6},{1,7},{2,4},{3,5},{4,2},{5,3},{6,0},{7,1},{8,14},{9,15},{10,... | collective-permute-start | bytes 208904 | tf_op jit(solution)/shard_map/ppermute | solution.py:272
  23.2 4.3 %collective-permute-start.7 = (f32[136,128]{1,0:T(8,128)S(1)}, f32[136,128]{1,0:T(8,128)S(1)}, u32[]{:S(2)}, u32[]{:S(2)}) collective-permute-start(f32[136,128]{1,0:T(8,128)S(1)} %add.27), channel_id=1, source_target_pairs={{0,4},{1,5},{2,6},{3,7},{4,0},{5,1},{6,2},{7,3},{8,12},{9,13},{10,... | collective-permute-start | bytes 208904 | tf_op jit(solution)/shard_map/ppermute | solution.py:272
  23.7 4.3 %collective-permute-start.6 = (f32[136,128]{1,0:T(8,128)S(1)}, f32[136,128]{1,0:T(8,128)S(1)}, u32[]{:S(2)}, u32[]{:S(2)}) collective-permute-start(f32[136,128]{1,0:T(8,128)S(1)} %add.27), channel_id=1, source_target_pairs={{0,2},{1,3},{2,0},{3,1},{4,6},{5,7},{6,4},{7,5},{8,10},{9,11},{10,... | collective-permute-start | bytes 208904 | tf_op jit(solution)/shard_map/ppermute | solution.py:272
  28.0 5.4 %collective-permute-start.9 = (f32[136,128]{1,0:T(8,128)S(1)}, f32[136,128]{1,0:T(8,128)S(1)}, u32[]{:S(2)}, u32[]{:S(2)}) collective-permute-start(f32[136,128]{1,0:T(8,128)S(1)} %add_add_fusion), channel_id=1, source_target_pairs={{0,8},{1,9},{2,10},{3,11},{4,12},{5,13},{6,14},{7,15},{8,0},{9,1},... | collective-permute-start | bytes 208904 | tf_op jit(solution)/shard_map/ppermute | solution.py:272
  33.4 1.3 %collective-permute-start.10 = (f32[136,128]{1,0:T(8,128)S(1)}, f32[136,128]{1,0:T(8,128)S(1)}, u32[]{:S(2)}, u32[]{:S(2)}) collective-permute-start(f32[136,128]{1,0:T(8,128)S(1)} %add.31.mine_ref), channel_id=1, source_target_pairs={{0,1},{1,0},{2,3},{3,2},{4,5},{5,4},{6,7},{7,6},{8,9},{9,8},{10,11... | collective-permute-start | bytes 208904 | tf_op jit(solution)/shard_map/ppermute | solution.py:275

commit v6 on v4

--- a/solution.py
+++ b/solution.py
@@ -28,7 +28,9 @@
 
 
 def mm3(a_high, a_low, b_high, b_low):
-    return mm(a_high, b_high) + (mm(a_high, b_low) + mm(a_low, b_high))
+    rows = a_high.shape[0]
+    both = mm(jnp.concatenate([a_high, a_low], axis=0), b_high)
+    return both[:rows] + (mm(a_high, b_low) + both[rows:])
 
 
 def prepare_kernel(total_blocks, cols_ref, *refs):

time: 36.7 us -> 36.7 us (level)
  no operation moved by 1% of the time
where the time goes in v6:
time: 36.7 us; the launch traced here: 36.5 us
  starting transfers between devices  18.2 us (50%)
  waiting for transfers between devices  10.9 us (30%)
  Pallas kernels  4.11 us (11%)
  local copies, waits for them, and re-layouts  2.52 us (7%)
  other arithmetic  0.77 us (2%)
    ppermute x2, starting transfers between devices, halo(): chip = lax.ppermute(block, 'row', chip_pairs)  9.94 us
    ppermute x4, starting transfers between devices, on_device(): lax.ppermute(total, 'row', [(i, i ^ step) for i in range(devices)])  6.21 us
    ppermute x4, waiting for transfers between devices, on_device(): lax.ppermute(total, 'row', [(i, i ^ step) for i in range(devices)])  6.09 us
    unnamed x12, local copies, waits for them, and re-layouts  2.52 us
    ppermute x1, waiting for transfers between devices, on_device(): moved = lax.ppermute(coef, 'node', [(i, i ^ shift) for i in range(nodes)])  1.85 us
    pallas_call x1, Pallas kernels, on_device(): call(functools.partial(finish_kernel, row_scale), jax.ShapeDtypeStruct((r...  1.76 us
    ppermute x1, starting transfers between devices, on_device(): moved = lax.ppermute(coef, 'node', [(i, i ^ shift) for i in range(nodes)])  1.49 us
    ppermute x1, waiting for transfers between devices, on_device(): theirs = lax.ppermute(total, 'row', core_pairs)  1.25 us
  transfers between devices with their start and end apart: 11, of which 9 were waited for; matrix products, arithmetic and copies ran while one was open for 2% of the time, Pallas kernels for 3%

profile of v6, /device:TPU:0, one launch (start us, length us, event | category | flops | bytes accessed | tf_op | source)
XLA Modules:
  0.0 36.5 jit_solution(993312219565141633)
XLA Ops:
  0.0 5.4 %collective-permute-start.1 = (f32[256,256]{1,0:T(8,128)}, f32[256,256]{1,0:T(8,128)S(1)}, u32[]{:S(2)}, u32[]{:S(2)}) collective-permute-start(f32[256,256]{1,0:T(8,128)} %start_ref.1), channel_id=1, source_target_pairs={{0,15},{1,2},{2,1},{3,4},{4,3},{5,6},{6,5},{7,8},{8,7},{9,10},{10,... | collective-permute-start | bytes 786440 | tf_op jit(solution)/shard_map/ppermute | solution.py:197
  5.4 0.0 collective-permute-start
  5.4 0.7 %fusion.2 = (f32[1,3]{1,0:T(1,128)S(1)}, f32[3]{0:T(128)S(1)}, f32[3]{0:T(128)S(1)}) fusion(s32[3]{0:T(128)} %param.15, f32[3]{0:T(128)} %param.14, f32[3]{0:T(128)} %param.13, f32[3]{0:T(128)} %param.11, f32[3]{0:T(128)} %param.12), kind=kLoop, calls=%fused_computation.6 | loop fusion | flops 66 | bytes 96 | tf_op jit(solution)/shard_map/broadcast_in_dim | solution.py:208
  6.2 0.0 copy-start.3
  6.2 0.0 copy-start.4
  6.2 0.0 copy-start.5
  6.2 0.6 %copy-done.3 = s32[3]{0:T(128)S(1)} copy-done((s32[3]{0:T(128)S(1)}, s32[3]{0:T(128)}, u32[]{:S(2)}) %copy-start.3) | copy-done | bytes 36
  6.8 0.0 copy-done.4
  6.9 0.0 copy-done.5
  6.9 0.0 copy-start.2
  6.9 0.7 %copy-done.2 = s32[2,7]{1,0:T(2,128)S(1)} copy-done((s32[2,7]{1,0:T(2,128)S(1)}, s32[2,7]{1,0:T(2,128)}, u32[]{:S(2)}) %copy-start.2) | copy-done | bytes 80
  7.6 0.0 copy-start.1
  7.6 1.2 %copy-done.1 = f32[2,7,128,128]{3,2,1,0:T(8,128)S(1)} copy-done((f32[2,7,128,128]{3,2,1,0:T(8,128)S(1)}, f32[2,7,128,128]{3,2,1,0:T(8,128)}, u32[]{:S(2)}) %copy-start.1) | copy-done | bytes 917528
  8.7 0.0 copy-start
  8.7 0.9 %prepare.1 = (bf16[256,768]{1,0:T(8,128)(2,1)S(1)}, bf16[256,768]{1,0:T(8,128)(2,1)S(1)}, s32[8,128]{1,0:T(8,128)S(1)}, f32[8,128]{1,0:T(8,128)S(1)}) custom-call(s32[2,7]{1,0:T(2,128)S(1)} %copy-done.2, f32[1,3]{1,0:T(1,128)S(1)} %get-tuple-element.27.refs_0_, f32[1,3]{1,0:T(1,128)S(1)} %get-tuple-element.26.refs_1_, f32[1,3]{1,0:T(1,128)S(1)} %get-tuple-element.23.refs_2_, ...), custom_call_target="tpu_custom_call" | custom-call | flops 917504 | bytes 2490368 | tf_op jit(solution)/shard_map/prepare/pallas_call | solution.py:215
  9.6 0.2 collective-permute-done.1.chip_ref
  9.8 0.0 collective-permute-done.core_ref
  9.8 0.0 copy-done
  9.8 0.5 %sweep.1.own_ref = f32[256,256]{1,0:T(8,128)S(1)} custom-call(bf16[256,768]{1,0:T(8,128)(2,1)S(1)} %get-tuple-element.14.high_ref, bf16[256,768]{1,0:T(8,128)(2,1)S(1)} %get-tuple-element.15.low_ref, f32[256,256]{1,0:T(8,128)S(1)} %copy-done, f32[256,256]{1,0:T(8,128)S(1)} %collective-permute-done.core_ref, f32[256,256]{1,0:T(8,128)S(1)} %collective-permute-done.1.chip_ref), custom_call_target="tpu_custom_call" | custom-call | flops 100663296 | bytes 1048576 | tf_op jit(solution)/shard_map/sweep/pallas_call | solution.py:239
  10.3 4.5 %collective-permute-start.3 = (f32[256,256]{1,0:T(8,128)S(1)}, f32[256,256]{1,0:T(8,128)S(1)}, u32[]{:S(2)}, u32[]{:S(2)}) collective-permute-start(f32[256,256]{1,0:T(8,128)S(1)} %sweep.1.own_ref), channel_id=1, source_target_pairs={{0,15},{1,2},{2,1},{3,4},{4,3},{5,6},{6,5},{7,8},{8,7},{9,10},{10,... | collective-permute-start | bytes 786440 | tf_op jit(solution)/shard_map/ppermute | solution.py:197
  14.8 0.0 collective-permute-start.2
  14.8 1.5 %collective-permute-start.4 = (f32[8,128]{1,0:T(8,128)S(1)}, f32[8,128]{1,0:T(8,128)S(1)}, u32[]{:S(2)}, u32[]{:S(2)}) collective-permute-start(f32[8,128]{1,0:T(8,128)S(1)} %get-tuple-element.18.coef_ref), channel_id=1, source_target_pairs={{0,16},{16,0},{1,17},{17,1},{2,18},{18,2},{3,19},{19,3},{4,20},{20... | collective-permute-start | bytes 12296 | tf_op jit(solution)/shard_map/ppermute | solution.py:247
  16.3 0.3 near.1.near_ref
  16.6 1.9 %collective-permute-done.4.other_ref = f32[8,128]{1,0:T(8,128)S(1)} collective-permute-done((f32[8,128]{1,0:T(8,128)S(1)}, f32[8,128]{1,0:T(8,128)S(1)}, u32[]{:S(2)}, u32[]{:S(2)}) %collective-permute-start.4) | collective-permute-done | bytes 4128 | tf_op jit(solution)/shard_map/ppermute | solution.py:247
  18.4 0.6 %collective-permute-done.3.chip_ref = f32[256,256]{1,0:T(8,128)S(1)} collective-permute-done((f32[256,256]{1,0:T(8,128)S(1)}, f32[256,256]{1,0:T(8,128)S(1)}, u32[]{:S(2)}, u32[]{:S(2)}) %collective-permute-start.3) | collective-permute-done | bytes 262176 | tf_op jit(solution)/shard_map/ppermute | solution.py:197
  19.0 0.0 collective-permute-done.2.core_ref
  19.0 0.8 %gram.1 = (f32[256,256]{1,0:T(8,128)S(1)}, f32[136,128]{1,0:T(8,128)S(1)}, f32[136,128]{1,0:T(8,128)S(1)}) custom-call(bf16[256,768]{1,0:T(8,128)(2,1)S(1)} %get-tuple-element.14.high_ref, bf16[256,768]{1,0:T(8,128)(2,1)S(1)} %get-tuple-element.15.low_ref, f32[256,256]{1,0:T(8,128)S(1)} %sweep.1.own_ref, f32[256,256]{1,0:T(8,128)S(1)} %near.1.near_ref, ...), custom_call_target="tpu_custom_call" | custom-call | flops 167772160 | bytes 2097152 | tf_op jit(solution)/shard_map/gram/pallas_call | solution.py:252
  19.7 0.4 %collective-permute-start.5 = (f32[136,128]{1,0:T(8,128)S(1)}, f32[136,128]{1,0:T(8,128)S(1)}, u32[]{:S(2)}, u32[]{:S(2)}) collective-permute-start(f32[136,128]{1,0:T(8,128)S(1)} %get-tuple-element.22), channel_id=1, source_target_pairs={{0,1},{1,0},{2,3},{3,2},{4,5},{5,4},{6,7},{7,6},{8,9},{9,8},{10,11... | collective-permute-start | bytes 208904 | tf_op jit(solution)/shard_map/ppermute | solution.py:261
  20.2 0.9 %collective-permute-done.5 = f32[136,128]{1,0:T(8,128)S(1)} collective-permute-done((f32[136,128]{1,0:T(8,128)S(1)}, f32[136,128]{1,0:T(8,128)S(1)}, u32[]{:S(2)}, u32[]{:S(2)}) %collective-permute-start.5) | collective-permute-done | bytes 69664 | tf_op jit(solution)/shard_map/ppermute | solution.py:261
  21.1 2.1 %collective-permute-start.8 = (f32[136,128]{1,0:T(8,128)S(1)}, f32[136,128]{1,0:T(8,128)S(1)}, u32[]{:S(2)}, u32[]{:S(2)}) collective-permute-start(f32[136,128]{1,0:T(8,128)S(1)} %add.27), channel_id=1, source_target_pairs={{0,6},{1,7},{2,4},{3,5},{4,2},{5,3},{6,0},{7,1},{8,14},{9,15},{10,... | collective-permute-start | bytes 208904 | tf_op jit(solution)/shard_map/ppermute | solution.py:266
  23.2 0.5 %collective-permute-start.7 = (f32[136,128]{1,0:T(8,128)S(1)}, f32[136,128]{1,0:T(8,128)S(1)}, u32[]{:S(2)}, u32[]{:S(2)}) collective-permute-start(f32[136,128]{1,0:T(8,128)S(1)} %add.27), channel_id=1, source_target_pairs={{0,4},{1,5},{2,6},{3,7},{4,0},{5,1},{6,2},{7,3},{8,12},{9,13},{10,... | collective-permute-start | bytes 208904 | tf_op jit(solution)/shard_map/ppermute | solution.py:266
  23.7 1.0 %collective-permute-start.6 = (f32[136,128]{1,0:T(8,128)S(1)}, f32[136,128]{1,0:T(8,128)S(1)}, u32[]{:S(2)}, u32[]{:S(2)}) collective-permute-start(f32[136,128]{1,0:T(8,128)S(1)} %add.27), channel_id=1, source_target_pairs={{0,2},{1,3},{2,0},{3,1},{4,6},{5,7},{6,4},{7,5},{8,10},{9,11},{10,... | collective-permute-start | bytes 208904 | tf_op jit(solution)/shard_map/ppermute | solution.py:266
  24.7 2.4 %collective-permute-done.8 = f32[136,128]{1,0:T(8,128)S(1)} collective-permute-done((f32[136,128]{1,0:T(8,128)S(1)}, f32[136,128]{1,0:T(8,128)S(1)}, u32[]{:S(2)}, u32[]{:S(2)}) %collective-permute-start.8) | collective-permute-done | bytes 69664 | tf_op jit(solution)/shard_map/ppermute | solution.py:266
  27.1 0.5 %collective-permute-done.7 = f32[136,128]{1,0:T(8,128)S(1)} collective-permute-done((f32[136,128]{1,0:T(8,128)S(1)}, f32[136,128]{1,0:T(8,128)S(1)}, u32[]{:S(2)}, u32[]{:S(2)}) %collective-permute-start.7) | collective-permute-done | bytes 69664 | tf_op jit(solution)/shard_map/ppermute | solution.py:266
  27.6 0.5 %collective-permute-done.6 = f32[136,128]{1,0:T(8,128)S(1)} collective-permute-done((f32[136,128]{1,0:T(8,128)S(1)}, f32[136,128]{1,0:T(8,128)S(1)}, u32[]{:S(2)}, u32[]{:S(2)}) %collective-permute-start.6) | collective-permute-done | bytes 69664 | tf_op jit(solution)/shard_map/ppermute | solution.py:266
  28.0 2.7 %collective-permute-start.9 = (f32[136,128]{1,0:T(8,128)S(1)}, f32[136,128]{1,0:T(8,128)S(1)}, u32[]{:S(2)}, u32[]{:S(2)}) collective-permute-start(f32[136,128]{1,0:T(8,128)S(1)} %add_add_fusion), channel_id=1, source_target_pairs={{0,8},{1,9},{2,10},{3,11},{4,12},{5,13},{6,14},{7,15},{8,0},{9,1},... | collective-permute-start | bytes 208904 | tf_op jit(solution)/shard_map/ppermute | solution.py:266
  30.7 2.7 %collective-permute-done.9 = f32[136,128]{1,0:T(8,128)S(1)} collective-permute-done((f32[136,128]{1,0:T(8,128)S(1)}, f32[136,128]{1,0:T(8,128)S(1)}, u32[]{:S(2)}, u32[]{:S(2)}) %collective-permute-start.9) | collective-permute-done | bytes 69664 | tf_op jit(solution)/shard_map/ppermute | solution.py:266
  33.4 0.1 collective-permute-start.10
  33.5 1.2 %collective-permute-done.10.theirs_ref = f32[136,128]{1,0:T(8,128)S(1)} collective-permute-done((f32[136,128]{1,0:T(8,128)S(1)}, f32[136,128]{1,0:T(8,128)S(1)}, u32[]{:S(2)}, u32[]{:S(2)}) %collective-permute-start.10) | collective-permute-done | bytes 69664 | tf_op jit(solution)/shard_map/ppermute | solution.py:269
  34.8 1.8 %finish.1 = f32[256,256]{1,0:T(8,128)} custom-call(f32[256,256]{1,0:T(8,128)S(1)} %get-tuple-element.20.filtered_ref, f32[136,128]{1,0:T(8,128)S(1)} %add.31.mine_ref, f32[136,128]{1,0:T(8,128)S(1)} %collective-permute-done.10.theirs_ref, s32[8,128]{1,0:T(8,128)S(1)} %get-tuple-element.19.odd_ref), custom_call_target="tpu_custom_call" | custom-call | flops 301989888 | bytes 786432 | tf_op jit(solution)/shard_map/finish/pallas_call | solution.py:271
  (4 shorter events, 0.0 us)
Async XLA Ops:
  0.0 9.8 %collective-permute-start.1 = (f32[256,256]{1,0:T(8,128)}, f32[256,256]{1,0:T(8,128)S(1)}, u32[]{:S(2)}, u32[]{:S(2)}) collective-permute-start(f32[256,256]{1,0:T(8,128)} %start_ref.1), channel_id=1, source_target_pairs={{0,15},{1,2},{2,1},{3,4},{4,3},{5,6},{6,5},{7,8},{8,7},{9,10},{10,... | collective-permute-start | bytes 786440 | tf_op jit(solution)/shard_map/ppermute | solution.py:197
  5.4 4.4 %collective-permute-start = (f32[256,256]{1,0:T(8,128)}, f32[256,256]{1,0:T(8,128)S(1)}, u32[]{:S(2)}, u32[]{:S(2)}) collective-permute-start(f32[256,256]{1,0:T(8,128)} %start_ref.1), channel_id=1, source_target_pairs={{0,1},{1,0},{2,3},{3,2},{4,5},{5,4},{6,7},{7,6},{8,9},{9,8},{10,11... | collective-permute-start | bytes 786440 | tf_op jit(solution)/shard_map/ppermute | solution.py:198
  6.2 0.7 %copy-start.3 = (s32[3]{0:T(128)S(1)}, s32[3]{0:T(128)}, u32[]{:S(2)}) copy-start(s32[3]{0:T(128)} %param.15) | copy-start | bytes 40
  6.2 0.7 %copy-start.4 = (f32[3]{0:T(128)S(1)}, f32[3]{0:T(128)}, u32[]{:S(2)}) copy-start(f32[3]{0:T(128)} %param.14) | copy-start | bytes 40
  6.2 0.7 %copy-start.5 = (f32[3]{0:T(128)S(1)}, f32[3]{0:T(128)}, u32[]{:S(2)}) copy-start(f32[3]{0:T(128)} %param.13) | copy-start | bytes 40
  6.9 0.7 %copy-start.2 = (s32[2,7]{1,0:T(2,128)S(1)}, s32[2,7]{1,0:T(2,128)}, u32[]{:S(2)}) copy-start(s32[2,7]{1,0:T(2,128)} %cols_ref.1) | copy-start | bytes 172
  7.6 1.2 %copy-start.1 = (f32[2,7,128,128]{3,2,1,0:T(8,128)S(1)}, f32[2,7,128,128]{3,2,1,0:T(8,128)}, u32[]{:S(2)}) copy-start(f32[2,7,128,128]{3,2,1,0:T(8,128)} %refs_3_.1) | copy-start | bytes 2752516
  8.7 1.1 %copy-start = (f32[256,256]{1,0:T(8,128)S(1)}, f32[256,256]{1,0:T(8,128)}, u32[]{:S(2)}) copy-start(f32[256,256]{1,0:T(8,128)} %start_ref.1) | copy-start | bytes 786436
  10.3 8.7 %collective-permute-start.3 = (f32[256,256]{1,0:T(8,128)S(1)}, f32[256,256]{1,0:T(8,128)S(1)}, u32[]{:S(2)}, u32[]{:S(2)}) collective-permute-start(f32[256,256]{1,0:T(8,128)S(1)} %sweep.1.own_ref), channel_id=1, source_target_pairs={{0,15},{1,2},{2,1},{3,4},{4,3},{5,6},{6,5},{7,8},{8,7},{9,10},{10,... | collective-permute-start | bytes 786440 | tf_op jit(solution)/shard_map/ppermute | solution.py:197
  14.8 4.2 %collective-permute-start.2 = (f32[256,256]{1,0:T(8,128)S(1)}, f32[256,256]{1,0:T(8,128)S(1)}, u32[]{:S(2)}, u32[]{:S(2)}) collective-permute-start(f32[256,256]{1,0:T(8,128)S(1)} %sweep.1.own_ref), channel_id=1, source_target_pairs={{0,1},{1,0},{2,3},{3,2},{4,5},{5,4},{6,7},{7,6},{8,9},{9,8},{10,11... | collective-permute-start | bytes 786440 | tf_op jit(solution)/shard_map/ppermute | solution.py:198
  14.8 3.6 %collective-permute-start.4 = (f32[8,128]{1,0:T(8,128)S(1)}, f32[8,128]{1,0:T(8,128)S(1)}, u32[]{:S(2)}, u32[]{:S(2)}) collective-permute-start(f32[8,128]{1,0:T(8,128)S(1)} %get-tuple-element.18.coef_ref), channel_id=1, source_target_pairs={{0,16},{16,0},{1,17},{17,1},{2,18},{18,2},{3,19},{19,3},{4,20},{20... | collective-permute-start | bytes 12296 | tf_op jit(solution)/shard_map/ppermute | solution.py:247
  19.7 1.4 %collective-permute-start.5 = (f32[136,128]{1,0:T(8,128)S(1)}, f32[136,128]{1,0:T(8,128)S(1)}, u32[]{:S(2)}, u32[]{:S(2)}) collective-permute-start(f32[136,128]{1,0:T(8,128)S(1)} %get-tuple-element.22), channel_id=1, source_target_pairs={{0,1},{1,0},{2,3},{3,2},{4,5},{5,4},{6,7},{7,6},{8,9},{9,8},{10,11... | collective-permute-start | bytes 208904 | tf_op jit(solution)/shard_map/ppermute | solution.py:261
  21.1 6.0 %collective-permute-start.8 = (f32[136,128]{1,0:T(8,128)S(1)}, f32[136,128]{1,0:T(8,128)S(1)}, u32[]{:S(2)}, u32[]{:S(2)}) collective-permute-start(f32[136,128]{1,0:T(8,128)S(1)} %add.27), channel_id=1, source_target_pairs={{0,6},{1,7},{2,4},{3,5},{4,2},{5,3},{6,0},{7,1},{8,14},{9,15},{10,... | collective-permute-start | bytes 208904 | tf_op jit(solution)/shard_map/ppermute | solution.py:266
  23.2 4.3 %collective-permute-start.7 = (f32[136,128]{1,0:T(8,128)S(1)}, f32[136,128]{1,0:T(8,128)S(1)}, u32[]{:S(2)}, u32[]{:S(2)}) collective-permute-start(f32[136,128]{1,0:T(8,128)S(1)} %add.27), channel_id=1, source_target_pairs={{0,4},{1,5},{2,6},{3,7},{4,0},{5,1},{6,2},{7,3},{8,12},{9,13},{10,... | collective-permute-start | bytes 208904 | tf_op jit(solution)/shard_map/ppermute | solution.py:266
  23.7 4.3 %collective-permute-start.6 = (f32[136,128]{1,0:T(8,128)S(1)}, f32[136,128]{1,0:T(8,128)S(1)}, u32[]{:S(2)}, u32[]{:S(2)}) collective-permute-start(f32[136,128]{1,0:T(8,128)S(1)} %add.27), channel_id=1, source_target_pairs={{0,2},{1,3},{2,0},{3,1},{4,6},{5,7},{6,4},{7,5},{8,10},{9,11},{10,... | collective-permute-start | bytes 208904 | tf_op jit(solution)/shard_map/ppermute | solution.py:266
  28.0 5.4 %collective-permute-start.9 = (f32[136,128]{1,0:T(8,128)S(1)}, f32[136,128]{1,0:T(8,128)S(1)}, u32[]{:S(2)}, u32[]{:S(2)}) collective-permute-start(f32[136,128]{1,0:T(8,128)S(1)} %add_add_fusion), channel_id=1, source_target_pairs={{0,8},{1,9},{2,10},{3,11},{4,12},{5,13},{6,14},{7,15},{8,0},{9,1},... | collective-permute-start | bytes 208904 | tf_op jit(solution)/shard_map/ppermute | solution.py:266
  33.4 1.3 %collective-permute-start.10 = (f32[136,128]{1,0:T(8,128)S(1)}, f32[136,128]{1,0:T(8,128)S(1)}, u32[]{:S(2)}, u32[]{:S(2)}) collective-permute-start(f32[136,128]{1,0:T(8,128)S(1)} %add.31.mine_ref), channel_id=1, source_target_pairs={{0,1},{1,0},{2,3},{3,2},{4,5},{5,4},{6,7},{7,6},{8,9},{9,8},{10,11... | collective-permute-start | bytes 208904 | tf_op jit(solution)/shard_map/ppermute | solution.py:269
